TPU v7x, 32 devices: a whole 2x2x4 slice. The times are simulated.
32 devices in a mesh: depth: 8 (over y, x, core), tile: 4 (over z).
Axes of the slice: x: 2, y: 2, z: 4, core: 2. Of those that a mesh axis runs over, the one named last changes fastest.
Arguments:
- coarse: bfloat16 [16, 32, 256], P('depth', None, 'tile'), may hold values from -6 to 6
- residual: bfloat16 [32, 64, 512], P('depth', None, 'tile'), may hold values from -6 to 6
- levels: int32 [8, 16, 128], P('depth', None, 'tile'), may hold values from 0 to 2
- slab_rank: int32 [8], replicated, may hold values from -8 to 7, as said below
- light_angles: float32 [2], replicated, may hold values from -3.140625 to 3.140625
- color_slope: float32 [3], replicated, may hold values from 0.5 to 2
- color_shift: float32 [3], replicated, may hold values from -1 to 1
Outputs:
- image: float32 [4, 64, 512], P(None, 'depth', 'tile')
- slab_shade: float32 [8, 64, 512], P('depth', None, 'tile')
Inputs may be any that keep to these rules, and one draw needn't show every extreme that they name: With p = s for every slab s, or p = 7 - s for every slab s, and one whole number c of 1 to 4: slab_rank is p where p >= c and p - 8 where p < c.
All inputs are finite; a program needn't handle non-finite values.
Results may differ from a plain program's by a relative error of at most 0.00079.
Values may be sent and summed in bfloat16 or wider, within the bound.
A program may use at most 192 MiB of HBM per device.

v0:
```python
import jax
import jax.numpy as jnp
from jax import lax
from jax.sharding import PartitionSpec as P


def padded_2(block, sides, width):
    for axis, dim in sides:
        count = lax.axis_size(axis)
        forward = [(i, i + 1) for i in range(count - 1)]
        backward = [(target, source) for source, target in forward]
        low = lax.ppermute(
            lax.slice_in_dim(block, block.shape[dim] - width, None, axis=dim), axis, forward
        )
        high = lax.ppermute(lax.slice_in_dim(block, 0, width, axis=dim), axis, backward)
        block = jnp.concatenate([low, block, high], axis=dim)
    return block


def from_partner(block, axis, apart):
    count = lax.axis_size(axis)
    route = []
    for low in range(count):
        high = low | 1 << apart
        if high != low and high < count:
            route += [(low, high), (high, low)]
    return lax.ppermute(block, axis, route)


def refine_block(coarse_part, residual_part, level_part):
    dep, rows, cols = residual_part.shape
    lifted = coarse_part.astype(jnp.float32)[:, None, :, None, :, None]
    lifted = jnp.broadcast_to(lifted, (dep // 2, 2, rows // 2, 2, cols // 2, 2)).reshape(
        dep, rows, cols
    )
    nb = level_part.shape
    scaled = level_part.astype(jnp.float32)[:, None, :, None, :, None]
    scaled = jnp.broadcast_to(
        scaled, (nb[0], dep // nb[0], nb[1], rows // nb[1], nb[2], cols // nb[2])
    ).reshape(dep, rows, cols)
    return (lifted + 0.5 * scaled * residual_part.astype(jnp.float32)).astype(jnp.bfloat16)


def light_vector(angles):
    return jnp.stack(
        [
            jnp.sin(angles[1]),
            jnp.cos(angles[1]) * jnp.sin(angles[0]),
            jnp.cos(angles[1]) * jnp.cos(angles[0]),
        ]
    )


def render_slab(padded, ascending, step, light, slope, shift):
    f = padded.astype(jnp.float32)
    v = f[2:-2, 2:-2, 2:-2]
    grad_z = (
        f[:-4, 2:-2, 2:-2]
        - 8.0 * f[1:-3, 2:-2, 2:-2]
        + 8.0 * f[3:-1, 2:-2, 2:-2]
        - f[4:, 2:-2, 2:-2]
    ) / 12.0
    grad_y = (
        f[2:-2, :-4, 2:-2]
        - 8.0 * f[2:-2, 1:-3, 2:-2]
        + 8.0 * f[2:-2, 3:-1, 2:-2]
        - f[2:-2, 4:, 2:-2]
    ) / 12.0
    grad_x = (
        f[2:-2, 2:-2, :-4]
        - 8.0 * f[2:-2, 2:-2, 1:-3]
        + 8.0 * f[2:-2, 2:-2, 3:-1]
        - f[2:-2, 2:-2, 4:]
    ) / 12.0
    along = light[0] * grad_z + light[1] * grad_y + light[2] * grad_x
    shade = 0.25 + 0.75 * jnp.abs(along) / jnp.sqrt(
        grad_z * grad_z + grad_y * grad_y + grad_x * grad_x + 1.0
    )
    extinct = 4.0 * jax.nn.sigmoid(3.0 * (v - 1.5))
    running = jnp.cumsum(extinct, axis=0)
    total = running[-1]
    before = jnp.where(ascending, running - extinct, total - running)
    weight = jnp.exp(-step * before) * (1.0 - jnp.exp(-step * extinct)) * shade
    colors = [jnp.sum(weight * jax.nn.sigmoid(slope[k] * v + shift[k]), axis=0) for k in range(3)]
    return (jnp.stack(colors + [1.0 - jnp.exp(-step * total)]), jnp.mean(shade, axis=0))


def place_over(front, back):
    return front + (1.0 - front[3:4]) * back


def shards(coarse, residual, levels, slab_rank, light_angles, color_slope, color_shift):
    dep, rows, cols = residual.shape
    slabs = lax.axis_size("depth")
    me = lax.axis_index("depth")
    ascending = slab_rank[0] < slab_rank[slabs - 1]
    my_rank = lax.dynamic_index_in_dim(slab_rank, me, 0, keepdims=False)
    visible = (my_rank >= 0).astype(jnp.float32)
    refined = refine_block(coarse, residual, levels)
    padded = padded_2(refined, (("depth", 0), ("tile", 2)), 2)
    padded = jnp.pad(padded, ((0, 0), (2, 2), (0, 0)))
    step = 4.0 / (dep * slabs)
    slab_image, mean_shade = render_slab(
        padded, ascending, step, light_vector(light_angles), color_slope, color_shift
    )
    slab_image = slab_image * visible
    shade_block = mean_shade[None]
    row_dev = rows // slabs
    blocks = slab_image.reshape(4, slabs, row_dev, cols)
    current = blocks
    for bit_number in range(slabs.bit_length() - 1):
        halved = current.reshape(4, current.shape[1] // 2, 2, row_dev, cols)
        mine = me >> bit_number & 1
        keep = lax.dynamic_index_in_dim(halved, mine, 2, keepdims=False)
        other = lax.dynamic_index_in_dim(halved, 1 - mine, 2, keepdims=False)
        arrived = from_partner(other, "depth", bit_number)
        partner_front = (me ^ 1 << bit_number < me) == ascending
        current = jnp.where(partner_front, place_over(arrived, keep), place_over(keep, arrived))
    return (current.reshape(4, row_dev, cols), shade_block)


def solution(mesh):
    placed = (
        P("depth", None, "tile"),
        P("depth", None, "tile"),
        P("depth", None, "tile"),
        P(),
        P(),
        P(),
        P(),
    )
    return jax.shard_map(
        shards,
        mesh=mesh,
        in_specs=placed,
        out_specs=(P(None, "depth", "tile"), P("depth", None, "tile")),
        check_vma=False,
    )
```

profile of v0, /device:TPU:0, one launch (start us, length us, event | category | flops | bytes accessed | tf_op | source)
XLA Modules:
  0.0 48.2 jit_solution(178018390196639407)
XLA Ops:
  0.6 0.0 copy-start.1
  0.6 0.0 copy-start
  0.7 0.0 copy-start.3
  0.7 0.0 copy-start.4
  0.7 0.0 copy-start.2
  0.7 0.0 copy-start.5
  0.7 4.6 %broadcast_in_dim.6 = f32[2,2,32,2,64,2]{5,4,3,2,1,0:T(8,128)} broadcast(bf16[2,32,64]{2,1,0:T(8,128)(2,1)} %param.7), dimensions={0,2,4} | broadcast | bytes 139264 | tf_op jit(solution)/shard_map/broadcast_in_dim | solution.py:33
  5.3 6.9 %reshape.85 = f32[4,64,128]{2,1,0:T(8,128)S(1)} reshape(f32[2,2,32,2,64,2]{5,4,3,2,1,0:T(8,128)} %broadcast_in_dim.6) | data formatting | bytes 262144 | tf_op jit(solution)/shard_map/reshape | solution.py:33
  12.2 0.0 copy-done.1
  12.2 0.2 broadcast_in_dim.7
  12.4 0.6 %mul.214 = f32[64,128]{1,0:T(8,128)S(1)} reshape(f32[16,4,32,4]{3,2,1,0:T(8,128)S(1)} %broadcast_in_dim.7) | data formatting | bytes 65536 | tf_op jit(solution)/shard_map/mul | solution.py:41
  13.0 0.0 copy-done
  13.1 1.3 %collective-permute-start.1 = (bf16[2,64,128]{2,1,0:T(8,128)(2,1)S(1)}, bf16[2,64,128]{2,1,0:T(8,128)(2,1)S(1)}, u32[]{:S(2)}, u32[]{:S(2)}) collective-permute-start(bf16[2,64,128]{2,1,0:T(8,128)(2,1)S(1)} %get-tuple-element.12), channel_id=1, source_target_pairs={{4,0},{8,4},{12,8},{16,12},{20,16},{24,20},{28,24},{5,1},{9,5},{13... | collective-permute-start | bytes 98312 | tf_op jit(solution)/shard_map/ppermute | solution.py:15
  14.4 3.0 %collective-permute-start = (bf16[2,64,128]{2,1,0:T(8,128)(2,1)S(1)}, bf16[2,64,128]{2,1,0:T(8,128)(2,1)S(1)}, u32[]{:S(2)}, u32[]{:S(2)}) collective-permute-start(bf16[2,64,128]{2,1,0:T(8,128)(2,1)S(1)} %get-tuple-element.11), channel_id=1, source_target_pairs={{0,4},{4,8},{8,12},{12,16},{16,20},{20,24},{24,28},{1,5},{5,9},{9,... | collective-permute-start | bytes 98312 | tf_op jit(solution)/shard_map/ppermute | solution.py:12
  17.4 0.0 copy-done.3
  17.4 0.6 %fusion.35 = (f32[1]{0:T(128)}, f32[1]{0:T(128)}, f32[1]{0:T(128)}) fusion(f32[3]{0:T(128)S(1)} %copy-done.3), kind=kLoop, calls=%fused_computation.75 | loop fusion | bytes 24 | tf_op jit(solution)/shard_map/slice | solution.py:84
  18.0 0.0 copy-done.4
  18.0 0.7 %fusion.34 = (f32[1]{0:T(128)}, f32[1]{0:T(128)}, f32[1]{0:T(128)}) fusion(f32[3]{0:T(128)S(1)} %copy-done.4), kind=kLoop, calls=%fused_computation.74 | loop fusion | bytes 24 | tf_op jit(solution)/shard_map/slice | solution.py:84
  18.7 0.0 copy-done.2
  18.7 0.6 %fusion.33 = (s32[1]{0:T(128)}, s32[1]{0:T(128)}, s32[1]{0:T(128)}) fusion(s32[8]{0:T(128)S(1)} %copy-done.2, s32[]{:T(128)S(6)} %select_n.62), kind=kLoop, calls=%fused_computation.73 | loop fusion | bytes 28 | tf_op jit(solution)/shard_map/jit(dynamic_index_in_dim)/dynamic_slice | solution.py:97
  19.3 0.0 copy-done.5
  19.3 0.6 %fusion.36 = (f32[1]{0:T(128)}, f32[1]{0:T(128)}) fusion(f32[2]{0:T(128)S(1)} %copy-done.5), kind=kLoop, calls=%fused_computation.76 | loop fusion | bytes 16 | tf_op jit(solution)/shard_map/slice | solution.py:48
  22.7 0.0 collective-permute-done.1
  22.8 0.0 collective-permute-done
  22.8 0.1 fusion.31
  22.9 1.3 %collective-permute-start.3 = (bf16[8,64,2]{2,1,0:T(8,128)(2,1)S(1)}, bf16[8,64,2]{2,1,0:T(8,128)(2,1)S(1)}, u32[]{:S(2)}, u32[]{:S(2)}) collective-permute-start(bf16[8,64,2]{2,1,0:T(8,128)(2,1)S(1)} %get-tuple-element.10), channel_id=1, source_target_pairs={{1,0},{2,1},{3,2},{5,4},{6,5},{7,6},{9,8},{10,9},{11,10},{13,12},{... | collective-permute-start | bytes 6152 | tf_op jit(solution)/shard_map/ppermute | solution.py:15
  24.2 5.6 %collective-permute-start.2 = (bf16[8,64,2]{2,1,0:T(8,128)(2,1)S(1)}, bf16[8,64,2]{2,1,0:T(8,128)(2,1)S(1)}, u32[]{:S(2)}, u32[]{:S(2)}) collective-permute-start(bf16[8,64,2]{2,1,0:T(8,128)(2,1)S(1)} %get-tuple-element.9), channel_id=1, source_target_pairs={{0,1},{1,2},{2,3},{4,5},{5,6},{6,7},{8,9},{9,10},{10,11},{12,13},{... | collective-permute-start | bytes 6152 | tf_op jit(solution)/shard_map/ppermute | solution.py:12
  31.6 0.0 collective-permute-done.3
  31.7 1.7 %collective-permute-done.2 = bf16[8,64,2]{2,1,0:T(8,128)(2,1)S(1)} collective-permute-done((bf16[8,64,2]{2,1,0:T(8,128)(2,1)S(1)}, bf16[8,64,2]{2,1,0:T(8,128)(2,1)S(1)}, u32[]{:S(2)}, u32[]{:S(2)}) %collective-permute-start.2) | collective-permute-done | bytes 2080 | tf_op jit(solution)/shard_map/ppermute | solution.py:12
  33.3 0.3 fusion.1
  33.6 0.1 fusion.13
  33.8 0.5 fusion.30
  34.2 4.1 %multiply_reduce_fusion.2 = (f32[64,128]{1,0:T(8,128)S(1)}, f32[64,128]{1,0:T(8,128)S(1)}, f32[64,128]{1,0:T(8,128)S(1)}) fusion(f32[8,68,132]{2,1,0:T(8,128)S(1)} %fusion.1, f32[]{:T(128)} %bitcast.7, f32[]{:T(128)} %bitcast.6, f32[]{:T(128)} %bitcast.13, f32[]{:T(128)} %bitcast.12, f32[]{:T(128)} %bitcast.10, f32[]{:T(128)} %bitcast.9, ...), kind=kLoop, calls=%fused_computation.30 | loop fusion | flops 1122304 | bytes 524313 | tf_op jit(solution)/shard_map/reduce_sum | solution.py:84
  38.3 0.5 %collective-permute-start.4 = (f32[4,4,8,128]{3,2,1,0:T(8,128)S(1)}, f32[4,4,8,128]{3,2,1,0:T(8,128)S(1)}, u32[]{:S(2)}, u32[]{:S(2)}) collective-permute-start(f32[4,4,8,128]{3,2,1,0:T(8,128)S(1)} %dynamic-slice_bitcast_fusion), channel_id=1, source_target_pairs={{0,4},{4,0},{8,12},{12,8},{16,20},{20,16},{24,28},{28,24},{1,5},{5... | collective-permute-start | bytes 196616 | tf_op jit(solution)/shard_map/ppermute | solution.py:27
  38.8 0.6 %multiply_bitcast_fusion = f32[1,64,128]{2,1,0:T(8,128)} fusion(f32[64,128]{1,0:T(8,128)S(1)} %get-tuple-element.5), kind=kLoop, calls=%fused_computation.47 | loop fusion | flops 8192 | bytes 65536 | tf_op jit(solution)/shard_map/div | solution.py:85
  39.4 0.3 collective-permute-done.4
  39.8 2.0 %collective-permute-start.5 = (f32[4,2,8,128]{3,2,1,0:T(8,128)S(1)}, f32[4,2,8,128]{3,2,1,0:T(8,128)S(1)}, u32[]{:S(2)}, u32[]{:S(2)}) collective-permute-start(f32[4,2,8,128]{3,2,1,0:T(8,128)S(1)} %dynamic-slice_bitcast_fusion.1), channel_id=1, source_target_pairs={{0,8},{8,0},{4,12},{12,4},{16,24},{24,16},{20,28},{28,20},{1,9},{9... | collective-permute-start | bytes 98312 | tf_op jit(solution)/shard_map/ppermute | solution.py:27
  41.8 2.0 %collective-permute-done.5 = f32[4,2,8,128]{3,2,1,0:T(8,128)S(1)} collective-permute-done((f32[4,2,8,128]{3,2,1,0:T(8,128)S(1)}, f32[4,2,8,128]{3,2,1,0:T(8,128)S(1)}, u32[]{:S(2)}, u32[]{:S(2)}) %collective-permute-start.5) | collective-permute-done | bytes 32800 | tf_op jit(solution)/shard_map/ppermute | solution.py:27
  43.8 2.1 %collective-permute-start.6 = (f32[4,1,8,128]{3,2,1,0:T(8,128)S(1)}, f32[4,1,8,128]{3,2,1,0:T(8,128)S(1)}, u32[]{:S(2)}, u32[]{:S(2)}) collective-permute-start(f32[4,1,8,128]{3,2,1,0:T(8,128)S(1)} %constant_dynamic-slice_fusion), channel_id=1, source_target_pairs={{0,16},{16,0},{4,20},{20,4},{8,24},{24,8},{12,28},{28,12},{1,17},{... | collective-permute-start | bytes 49160 | tf_op jit(solution)/shard_map/ppermute | solution.py:27
  45.9 1.7 %collective-permute-done.6 = f32[4,1,8,128]{3,2,1,0:T(8,128)S(1)} collective-permute-done((f32[4,1,8,128]{3,2,1,0:T(8,128)S(1)}, f32[4,1,8,128]{3,2,1,0:T(8,128)S(1)}, u32[]{:S(2)}, u32[]{:S(2)}) %collective-permute-start.6) | collective-permute-done | bytes 16416 | tf_op jit(solution)/shard_map/ppermute | solution.py:27
  47.6 0.6 %select_bitcast_fusion = f32[4,8,128]{2,1,0:T(8,128)} fusion(f32[4,1,8,128]{3,2,1,0:T(8,128)S(1)} %collective-permute-done.6, f32[4,2,8,128]{3,2,1,0:T(8,128)S(1)} %fusion.19, s32[]{:T(128)S(6)} %select_n.70, f32[8,128]{1,0:T(8,128)S(1)} %fusion.24, f32[8,128]{1,0:T(8,128)S(1)} %fusion.25, pred[]{:T(512)S(6)} %eq.9), kind=kLoop, calls=%fused_computation.55 | loop fusion | flops 20480 | bytes 57349 | tf_op jit(solution)/shard_map/reshape | solution.py:119
  (17 shorter events, 0.2 us)
Async XLA Ops:
  0.6 11.5 %copy-start.1 = (s32[1,16,32]{2,1,0:T(8,128)S(1)}, s32[1,16,32]{2,1,0:T(8,128)}, u32[]{:S(2)}) copy-start(s32[1,16,32]{2,1,0:T(8,128)} %param.9) | copy-start | bytes 6148
  0.6 12.4 %copy-start = (bf16[4,64,128]{2,1,0:T(8,128)(2,1)S(1)}, bf16[4,64,128]{2,1,0:T(8,128)(2,1)}, u32[]{:S(2)}) copy-start(bf16[4,64,128]{2,1,0:T(8,128)(2,1)} %param.8) | copy-start | bytes 196612
  0.7 16.8 %copy-start.3 = (f32[3]{0:T(128)S(1)}, f32[3]{0:T(128)}, u32[]{:S(2)}) copy-start(f32[3]{0:T(128)} %param.13) | copy-start | bytes 40
  0.7 17.4 %copy-start.4 = (f32[3]{0:T(128)S(1)}, f32[3]{0:T(128)}, u32[]{:S(2)}) copy-start(f32[3]{0:T(128)} %param.12) | copy-start | bytes 40
  0.7 18.0 %copy-start.2 = (s32[8]{0:T(128)S(1)}, s32[8]{0:T(128)}, u32[]{:S(2)}) copy-start(s32[8]{0:T(128)} %param.10) | copy-start | bytes 100
  0.7 18.6 %copy-start.5 = (f32[2]{0:T(128)S(1)}, f32[2]{0:T(128)}, u32[]{:S(2)}) copy-start(f32[2]{0:T(128)} %param.11) | copy-start | bytes 28
  13.1 9.7 %collective-permute-start.1 = (bf16[2,64,128]{2,1,0:T(8,128)(2,1)S(1)}, bf16[2,64,128]{2,1,0:T(8,128)(2,1)S(1)}, u32[]{:S(2)}, u32[]{:S(2)}) collective-permute-start(bf16[2,64,128]{2,1,0:T(8,128)(2,1)S(1)} %get-tuple-element.12), channel_id=1, source_target_pairs={{4,0},{8,4},{12,8},{16,12},{20,16},{24,20},{28,24},{5,1},{9,5},{13... | collective-permute-start | bytes 98312 | tf_op jit(solution)/shard_map/ppermute | solution.py:15
  14.4 8.4 %collective-permute-start = (bf16[2,64,128]{2,1,0:T(8,128)(2,1)S(1)}, bf16[2,64,128]{2,1,0:T(8,128)(2,1)S(1)}, u32[]{:S(2)}, u32[]{:S(2)}) collective-permute-start(bf16[2,64,128]{2,1,0:T(8,128)(2,1)S(1)} %get-tuple-element.11), channel_id=1, source_target_pairs={{0,4},{4,8},{8,12},{12,16},{16,20},{20,24},{24,28},{1,5},{5,9},{9,... | collective-permute-start | bytes 98312 | tf_op jit(solution)/shard_map/ppermute | solution.py:12
  22.9 8.8 %collective-permute-start.3 = (bf16[8,64,2]{2,1,0:T(8,128)(2,1)S(1)}, bf16[8,64,2]{2,1,0:T(8,128)(2,1)S(1)}, u32[]{:S(2)}, u32[]{:S(2)}) collective-permute-start(bf16[8,64,2]{2,1,0:T(8,128)(2,1)S(1)} %get-tuple-element.10), channel_id=1, source_target_pairs={{1,0},{2,1},{3,2},{5,4},{6,5},{7,6},{9,8},{10,9},{11,10},{13,12},{... | collective-permute-start | bytes 6152 | tf_op jit(solution)/shard_map/ppermute | solution.py:15
  24.2 9.1 %collective-permute-start.2 = (bf16[8,64,2]{2,1,0:T(8,128)(2,1)S(1)}, bf16[8,64,2]{2,1,0:T(8,128)(2,1)S(1)}, u32[]{:S(2)}, u32[]{:S(2)}) collective-permute-start(bf16[8,64,2]{2,1,0:T(8,128)(2,1)S(1)} %get-tuple-element.9), channel_id=1, source_target_pairs={{0,1},{1,2},{2,3},{4,5},{5,6},{6,7},{8,9},{9,10},{10,11},{12,13},{... | collective-permute-start | bytes 6152 | tf_op jit(solution)/shard_map/ppermute | solution.py:12
  38.3 1.4 %collective-permute-start.4 = (f32[4,4,8,128]{3,2,1,0:T(8,128)S(1)}, f32[4,4,8,128]{3,2,1,0:T(8,128)S(1)}, u32[]{:S(2)}, u32[]{:S(2)}) collective-permute-start(f32[4,4,8,128]{3,2,1,0:T(8,128)S(1)} %dynamic-slice_bitcast_fusion), channel_id=1, source_target_pairs={{0,4},{4,0},{8,12},{12,8},{16,20},{20,16},{24,28},{28,24},{1,5},{5... | collective-permute-start | bytes 196616 | tf_op jit(solution)/shard_map/ppermute | solution.py:27
  39.8 4.0 %collective-permute-start.5 = (f32[4,2,8,128]{3,2,1,0:T(8,128)S(1)}, f32[4,2,8,128]{3,2,1,0:T(8,128)S(1)}, u32[]{:S(2)}, u32[]{:S(2)}) collective-permute-start(f32[4,2,8,128]{3,2,1,0:T(8,128)S(1)} %dynamic-slice_bitcast_fusion.1), channel_id=1, source_target_pairs={{0,8},{8,0},{4,12},{12,4},{16,24},{24,16},{20,28},{28,20},{1,9},{9... | collective-permute-start | bytes 98312 | tf_op jit(solution)/shard_map/ppermute | solution.py:27
  43.8 3.8 %collective-permute-start.6 = (f32[4,1,8,128]{3,2,1,0:T(8,128)S(1)}, f32[4,1,8,128]{3,2,1,0:T(8,128)S(1)}, u32[]{:S(2)}, u32[]{:S(2)}) collective-permute-start(f32[4,1,8,128]{3,2,1,0:T(8,128)S(1)} %constant_dynamic-slice_fusion), channel_id=1, source_target_pairs={{0,16},{16,0},{4,20},{20,4},{8,24},{24,8},{12,28},{28,12},{1,17},{... | collective-permute-start | bytes 49160 | tf_op jit(solution)/shard_map/ppermute | solution.py:27
where the time goes:
time: 48.6 us; the launch traced here: 48.2 us
  starting transfers between devices  15.8 us (33%)
  local copies, waits for them, and re-layouts  15 us (31%)
  other arithmetic  6.27 us (13%)
  waiting for transfers between devices  5.69 us (12%)
  between operations  5.54 us (11%)
    ppermute x2, starting transfers between devices, padded_2(): lax.ppermute(lax.slice_in_dim(block, block.shape[dim] - width, None, axis...  8.6 us
    reshape x1, local copies, waits for them, and re-layouts, refine_block(): jnp.broadcast_to(lifted, (dep // 2, 2, rows // 2, 2, cols // 2, 2))  6.89 us
    ppermute x3, starting transfers between devices, from_partner(): return lax.ppermute(block, axis, route)  4.6 us
    broadcast_in_dim x1, local copies, waits for them, and re-layouts, refine_block(): jnp.broadcast_to(lifted, (dep // 2, 2, rows // 2, 2, cols // 2, 2))  4.58 us
    reduce_sum x1, other arithmetic, render_slab(): jnp.sum(weight * jax.nn.sigmoid(slope[k] * v + shift[k]), axis=0)  4.07 us
    ppermute x3, waiting for transfers between devices, from_partner(): return lax.ppermute(block, axis, route)  3.98 us
    ppermute x2, starting transfers between devices, padded_2(): lax.ppermute(lax.slice_in_dim(block, 0, width, axis=dim), axis, backward)  2.58 us
    ppermute x2, waiting for transfers between devices, padded_2(): lax.ppermute(lax.slice_in_dim(block, block.shape[dim] - width, None, axis...  1.68 us
  transfers between devices with their start and end apart: 7, of which 4 were waited for; matrix products, arithmetic and copies ran while one was open for 6% of the time, Pallas kernels for 0%

commit v1 on v0

v1 whole, which is shorter than its diff:
```python
import functools

import jax
import jax.numpy as jnp
from jax import lax
from jax.experimental import pallas as pl
from jax.experimental.pallas import tpu as pltpu
from jax.sharding import PartitionSpec as P

SUB = 8
HALO = 2


def each(count, body):
    if count == 1:
        body(0)
    else:
        lax.fori_loop(0, count, lambda i, _: (body(i), 0)[1], 0)


def repeat_matrix(shape, dim):
    factor = shape[dim] // shape[1 - dim]
    long = lax.broadcasted_iota(jnp.int32, shape, dim)
    short = lax.broadcasted_iota(jnp.int32, shape, 1 - dim) * factor
    return ((long >= short) & (long < short + factor)).astype(jnp.float32).astype(jnp.bfloat16)


def stencil_matrix(cols):
    apart = lax.broadcasted_iota(jnp.int32, (cols, cols), 0) - lax.broadcasted_iota(
        jnp.int32, (cols, cols), 1
    )
    value = jnp.where(apart == -2, 1.0, 0.0)
    value = jnp.where(apart == -1, -8.0, value)
    value = jnp.where(apart == 1, 8.0, value)
    value = jnp.where(apart == 2, -1.0, value)
    return value.astype(jnp.bfloat16)


def matmul(a, b):
    return jnp.dot(a, b, preferred_element_type=jnp.float32)


def kernel(
    slabs,
    tiles,
    coarse_in,
    residual_in,
    levels_in,
    rank_in,
    angles_in,
    slope_in,
    shift_in,
    image_out,
    shade_out,
    coarse,
    residual,
    levels,
    rank,
    angles,
    slope,
    shift,
    field16,
    field,
    low_halo,
    high_halo,
    edge,
    edge_left,
    edge_right,
    grad_x,
    grad_y,
    grad_z,
    tinted,
    pieces,
    arrived,
    shade_sum,
    image,
    load_sem,
    halo_send,
    halo_recv,
    piece_send,
    piece_recv,
    out_sem,
):
    dep, rows, cols = residual.shape
    me = lax.axis_index("depth")
    tile = lax.axis_index("tile")
    row_dev = rows // slabs
    per_piece = row_dev // SUB
    n_chunks = rows // SUB
    inner = min(n_chunks, cols // 4 // dep)
    n_blocks = n_chunks // inner
    block = inner * SUB
    step = 4.0 / (dep * slabs)

    barrier = pltpu.get_barrier_semaphore()
    for k in range(1, slabs):
        pl.semaphore_signal(
            barrier,
            inc=1,
            device_id=(lax.rem(me + k, slabs), tile),
            device_id_type=pl.DeviceIdType.MESH,
        )

    @pl.when(tile > 0)
    def _():
        pl.semaphore_signal(
            barrier, inc=1, device_id=(me, tile - 1), device_id_type=pl.DeviceIdType.MESH
        )

    @pl.when(tile < tiles - 1)
    def _():
        pl.semaphore_signal(
            barrier, inc=1, device_id=(me, tile + 1), device_id_type=pl.DeviceIdType.MESH
        )

    loads = [
        pltpu.make_async_copy(source, target, load_sem.at[i])
        for i, (source, target) in enumerate(
            [
                (residual_in, residual),
                (coarse_in, coarse),
                (levels_in, levels),
                (rank_in, rank),
                (angles_in, angles),
                (slope_in, slope),
                (shift_in, shift),
            ]
        )
    ]
    for load in loads:
        load.start()

    up_c = repeat_matrix((coarse.shape[2], cols), 1)
    up_r = repeat_matrix((rows, coarse.shape[1]), 0)
    level_c = repeat_matrix((levels.shape[2], cols), 1)
    level_r = repeat_matrix((rows, levels.shape[1]), 0)
    stencil = stencil_matrix(cols)
    lane = lax.broadcasted_iota(jnp.int32, (SUB, cols), 1)
    for z in range(dep):
        field[HALO + z, pl.ds(0, SUB), :] = jnp.zeros((SUB, cols), jnp.float32)
        field[HALO + z, pl.ds(SUB + rows, SUB), :] = jnp.zeros((SUB, cols), jnp.float32)
    for load in loads[1:]:
        load.wait()
    lifted = [
        matmul(up_r, matmul(coarse[z], up_c).astype(jnp.bfloat16)) for z in range(coarse.shape[0])
    ]
    scaled = [
        matmul(
            level_r,
            matmul((0.5 * levels[z].astype(jnp.float32)).astype(jnp.bfloat16), level_c).astype(
                jnp.bfloat16
            ),
        )
        for z in range(levels.shape[0])
    ]
    loads[0].wait()
    for z in range(dep):
        value = lifted[z * coarse.shape[0] // dep] + scaled[
            z * levels.shape[0] // dep
        ] * residual[z].astype(jnp.float32)
        rounded = value.astype(jnp.bfloat16)
        field16[z] = rounded
        field[HALO + z, pl.ds(SUB, rows), :] = rounded.astype(jnp.float32)

    def rows_of(q, i):
        start = q * block + i * SUB
        return start if isinstance(start, int) else pl.multiple_of(start, SUB)

    def pack(q):
        packed = jnp.zeros((SUB, cols), jnp.float32)
        for i in range(inner):
            for z in range(dep):
                j = i * dep + z
                value = field[HALO + z, pl.ds(SUB + rows_of(q, i), SUB), :]
                turned = pltpu.roll(value, (4 * j + HALO) % cols, 1)
                packed = jnp.where((lane >> 2) == j, turned, packed)
        edge[q] = packed

    each(n_blocks, pack)

    copies = [
        pltpu.make_async_remote_copy(
            source,
            target,
            halo_send.at[i],
            halo_recv.at[i],
            device_id=to,
            device_id_type=pl.DeviceIdType.MESH,
        )
        for i, (source, target, to) in enumerate(
            [
                (field16.at[pl.ds(dep - HALO, HALO)], low_halo, (me + 1, tile)),
                (field16.at[pl.ds(0, HALO)], high_halo, (me - 1, tile)),
                (edge, edge_left, (me, tile + 1)),
                (edge, edge_right, (me, tile - 1)),
            ]
        )
    ]
    can_send = [me < slabs - 1, me > 0, tile < tiles - 1, tile > 0]
    can_take = [me > 0, me < slabs - 1, tile > 0, tile < tiles - 1]
    landing = [low_halo, high_halo, edge_left, edge_right]

    pl.semaphore_wait(
        barrier, slabs - 1 + (tile > 0).astype(jnp.int32) + (tile < tiles - 1).astype(jnp.int32)
    )
    for copy, allowed in zip(copies, can_send):
        pl.when(allowed)(copy.start)
    for target, allowed in zip(landing, can_take):

        @pl.when(jnp.logical_not(allowed))
        def _():
            target[...] = jnp.zeros(target.shape, target.dtype)

    ascending = rank[0] < rank[slabs - 1]
    visible = jnp.where(rank[me] >= 0, 1.0, 0.0)
    azimuth = jnp.full((SUB, cols), angles[0], jnp.float32)
    elevation = jnp.full((SUB, cols), angles[1], jnp.float32)
    light_z = jnp.sin(elevation)
    light_y = jnp.cos(elevation) * jnp.sin(azimuth)
    light_x = jnp.cos(elevation) * jnp.cos(azimuth)

    for z in range(dep):
        grad_x[z] = matmul(field16[z], stencil)

    def halo_free(q):
        for i in range(inner):
            start = rows_of(q, i)
            here = pl.ds(start, SUB)
            value = [field[HALO + z, pl.ds(SUB + start, SUB), :] for z in range(dep)]
            for z in range(dep):

                def at(dy):
                    return field[HALO + z, pl.ds(SUB + start + dy, SUB), :]

                grad_y[z, here, :] = (at(-2) - at(2)) + 8.0 * (at(1) - at(-1))
                part = jnp.zeros((SUB, cols), jnp.float32)
                for dz, factor in ((-2, 1.0), (-1, -8.0), (1, 8.0), (2, -1.0)):
                    if 0 <= z + dz < dep:
                        part = part + factor * value[z + dz]
                grad_z[z, here, :] = part
            passed = [jnp.exp(-step * (2.0 + 2.0 * jnp.tanh(1.5 * (v - 1.5)))) for v in value]
            up, down = [None] * dep, [None] * dep
            up[0] = down[dep - 1] = jnp.ones((SUB, cols), jnp.float32)
            for z in range(1, dep):
                up[z] = up[z - 1] * passed[z - 1]
                down[dep - 1 - z] = down[dep - z] * passed[dep - z]
            for z in range(dep):
                weight = jnp.where(ascending, up[z], down[z]) * (1.0 - passed[z]) * visible
                for k in range(3):
                    colour = 0.5 + 0.5 * jnp.tanh(0.5 * (slope[k] * value[z] + shift[k]))
                    tinted[k, z, here, :] = weight * colour
            chunk = q * inner + i
            pieces[chunk // per_piece, 3, pl.ds(chunk % per_piece * SUB, SUB), :] = (
                1.0 - up[dep - 1] * passed[dep - 1]
            ) * visible

    each(n_blocks, halo_free)

    for copy, allowed in zip(copies, can_take):
        pl.when(allowed)(copy.wait_recv)

    def finish(q):
        left, right = edge_left[q], edge_right[q]
        place = lane & 3
        both = jnp.where(place < 2, left, right)
        outer = jnp.where(place < 2, -pltpu.roll(both, cols - 2, 1), pltpu.roll(both, 2, 1))
        near = jnp.where(
            place == 1,
            pltpu.roll(both, cols - 1, 1),
            jnp.where(place == 2, -pltpu.roll(both, 1, 1), 0.0),
        )
        fix = outer + 8.0 * near
        at_edge = (lane < HALO) | (lane >= cols - HALO)
        whole = q * block
        whole = whole if isinstance(whole, int) else pl.multiple_of(whole, block)
        low = [low_halo[z, pl.ds(whole, block), :].astype(jnp.float32) for z in range(HALO)]
        high = [high_halo[z, pl.ds(whole, block), :].astype(jnp.float32) for z in range(HALO)]
        for i in range(inner):
            here = pl.ds(rows_of(q, i), SUB)
            low_i = [v[i * SUB : (i + 1) * SUB] for v in low]
            high_i = [v[i * SUB : (i + 1) * SUB] for v in high]
            shades = []
            for z in range(dep):
                j = i * dep + z
                gx = grad_x[z, here, :] + jnp.where(
                    at_edge, pltpu.roll(fix, (cols - HALO - 4 * j) % cols, 1), 0.0
                )
                gy = grad_y[z, here, :]
                gz = grad_z[z, here, :]
                if z - 2 < 0:
                    gz = gz + low_i[z]
                if z - 1 < 0:
                    gz = gz - 8.0 * low_i[z + 1]
                if z + 1 >= dep:
                    gz = gz + 8.0 * high_i[z + 1 - dep]
                if z + 2 >= dep:
                    gz = gz - high_i[z + 2 - dep]
                along = light_z * gz + light_y * gy + light_x * gx
                square = gz * gz + gy * gy + gx * gx + 144.0
                shades.append(0.25 + 0.75 * jnp.abs(along) * lax.rsqrt(square))
            shade_sum[0, here, :] = sum(shades) * (1.0 / dep)
            chunk = q * inner + i
            for k in range(3):
                total = sum(tinted[k, z, here, :] * shades[z] for z in range(dep))
                pieces[chunk // per_piece, k, pl.ds(chunk % per_piece * SUB, SUB), :] = total

    each(n_blocks, finish)

    def piece_copy(other, slot):
        return pltpu.make_async_remote_copy(
            pieces.at[other],
            arrived.at[slot],
            piece_send.at[other],
            piece_recv.at[slot],
            device_id=(other, tile),
            device_id_type=pl.DeviceIdType.MESH,
        )

    others = [lax.rem(me + k, slabs) for k in range(1, slabs)]
    for other in others:
        piece_copy(other, me).start()
    shade_copy = pltpu.make_async_copy(shade_sum, shade_out, out_sem.at[0])
    shade_copy.start()
    arrived[me] = pieces[me]
    for other in others:
        piece_copy(other, other).wait_recv()
    total = [jnp.zeros((row_dev, cols), jnp.float32) for _ in range(3)]
    through = jnp.ones((row_dev, cols), jnp.float32)
    for s in range(slabs):
        layer = [
            jnp.where(ascending, arrived[s, k], arrived[slabs - 1 - s, k]) for k in range(4)
        ]
        total = [total[k] + through * layer[k] for k in range(3)]
        through = through * (1.0 - layer[3])
    for k in range(3):
        image[k] = total[k]
    image[3] = 1.0 - through
    image_copy = pltpu.make_async_copy(image, image_out, out_sem.at[1])
    image_copy.start()
    for copy, allowed in zip(copies, can_send):
        pl.when(allowed)(copy.wait_send)
    for other in others:
        piece_copy(other, me).wait_send()
    shade_copy.wait()
    image_copy.wait()


def shards(coarse, residual, levels, slab_rank, light_angles, color_slope, color_shift):
    dep, rows, cols = residual.shape
    slabs, tiles = lax.axis_size("depth"), lax.axis_size("tile")
    row_dev = rows // slabs
    n_chunks = rows // SUB
    n_blocks = n_chunks // min(n_chunks, cols // 4 // dep)
    f32, bf16 = jnp.float32, jnp.bfloat16
    hbm = pl.BlockSpec(memory_space=pl.ANY)
    dma = pltpu.SemaphoreType.DMA
    return pl.pallas_call(
        functools.partial(kernel, slabs, tiles),
        out_shape=(
            jax.ShapeDtypeStruct((4, row_dev, cols), f32),
            jax.ShapeDtypeStruct((1, rows, cols), f32),
        ),
        in_specs=[hbm] * 7,
        out_specs=(hbm, hbm),
        scratch_shapes=[
            pltpu.VMEM(coarse.shape, bf16),
            pltpu.VMEM(residual.shape, bf16),
            pltpu.VMEM(levels.shape, jnp.int32),
            pltpu.SMEM(slab_rank.shape, jnp.int32),
            pltpu.SMEM(light_angles.shape, f32),
            pltpu.SMEM(color_slope.shape, f32),
            pltpu.SMEM(color_shift.shape, f32),
            pltpu.VMEM((dep, rows, cols), bf16),
            pltpu.VMEM((dep + 2 * HALO, rows + 2 * SUB, cols), f32),
            pltpu.VMEM((HALO, rows, cols), bf16),
            pltpu.VMEM((HALO, rows, cols), bf16),
            pltpu.VMEM((n_blocks, SUB, cols), f32),
            pltpu.VMEM((n_blocks, SUB, cols), f32),
            pltpu.VMEM((n_blocks, SUB, cols), f32),
            pltpu.VMEM((dep, rows, cols), f32),
            pltpu.VMEM((dep, rows, cols), f32),
            pltpu.VMEM((dep, rows, cols), f32),
            pltpu.VMEM((3, dep, rows, cols), f32),
            pltpu.VMEM((slabs, 4, row_dev, cols), f32),
            pltpu.VMEM((slabs, 4, row_dev, cols), f32),
            pltpu.VMEM((1, rows, cols), f32),
            pltpu.VMEM((4, row_dev, cols), f32),
            dma((7,)),
            dma((4,)),
            dma((4,)),
            dma((slabs,)),
            dma((slabs,)),
            dma((2,)),
        ],
        compiler_params=pltpu.CompilerParams(
            collective_id=0, has_side_effects=True, vmem_limit_bytes=40 * 1024 * 1024
        ),
    )(coarse, residual, levels, slab_rank, light_angles, color_slope, color_shift)


def solution(mesh):
    placed = (
        P("depth", None, "tile"),
        P("depth", None, "tile"),
        P("depth", None, "tile"),
        P(),
        P(),
        P(),
        P(),
    )
    return jax.shard_map(
        shards,
        mesh=mesh,
        in_specs=placed,
        out_specs=(P(None, "depth", "tile"), P("depth", None, "tile")),
        check_vma=False,
    )
```

time: 48.6 us -> 18 us (0.37)
  starting transfers between devices: 15.8 us -> 0 us
  Pallas kernels: 0 us -> 10.9 us
  local copies, waits for them, and re-layouts: 15 us -> 6.09 us
  other arithmetic: 6.27 us -> 0 us
  waiting for transfers between devices: 5.69 us -> 0 us
  between operations: 5.54 us -> 0.66 us
    ppermute x7 -> x0, starting transfers between devices: 15.8 us -> none  [the longest x2 8.6 us: padded_2(): lax.ppermute(lax.slice_in_dim(block, block.shape[dim] - width, None, axis...]
    pallas_call x0 -> x1, Pallas kernels: none -> 10.9 us  [shards(): pl.pallas_call(functools.partial(kernel, slabs, tiles), out_shape=(jax.Sh...]
    reshape x1 -> x0, local copies, waits for them, and re-layouts: 6.89 us -> none  [refine_block(): jnp.broadcast_to(lifted, (dep // 2, 2, rows // 2, 2, cols // 2, 2))]
    unnamed x12 -> x16, local copies, waits for them, and re-layouts: 0.03 us -> 6.09 us
    ppermute x7 -> x0, waiting for transfers between devices: 5.69 us -> none  [the longest x3 3.98 us: from_partner(): return lax.ppermute(block, axis, route)]
    broadcast_in_dim x2 -> x0, local copies, waits for them, and re-layouts: 4.76 us -> none  [the longest x1 4.58 us: refine_block(): jnp.broadcast_to(lifted, (dep // 2, 2, rows // 2, 2, cols // 2, 2))]
    reduce_sum x2 -> x0, other arithmetic: 4.53 us -> none  [the longest x1 4.07 us: render_slab(): jnp.sum(weight * jax.nn.sigmoid(slope[k] * v + shift[k]), axis=0)]
    slice x5 -> x0, local copies, waits for them, and re-layouts: 2 us -> none  [the longest x1 0.65 us: render_slab(): slope[k] * v + shift[k]]
  transfers between devices with their start and end apart: 7 -> 0, of which waited for: 4 -> 0; matrix products, arithmetic and copies ran while one was open for 6% -> 0% of each run, Pallas kernels for 0% -> 0%
where the time goes in v1:
time: 18 us; the launch traced here: 17.7 us
  Pallas kernels  10.9 us (61%)
  local copies, waits for them, and re-layouts  6.09 us (34%)
  between operations  0.66 us (4%)
    pallas_call x1, Pallas kernels, shards(): pl.pallas_call(functools.partial(kernel, slabs, tiles), out_shape=(jax.Sh...  10.9 us
    unnamed x16, local copies, waits for them, and re-layouts  6.09 us

profile of v1, /device:TPU:0, one launch (start us, length us, event | category | flops | bytes accessed | tf_op | source)
XLA Modules:
  0.0 17.7 jit_solution(17980586376288634106)
XLA Ops:
  0.6 0.0 copy-start
  0.6 0.8 %copy-done = bf16[4,64,128]{2,1,0:T(8,128)(2,1)S(1)} copy-done((bf16[4,64,128]{2,1,0:T(8,128)(2,1)S(1)}, bf16[4,64,128]{2,1,0:T(8,128)(2,1)}, u32[]{:S(2)}) %copy-start) | copy-done | bytes 65560
  1.5 0.0 copy-start.1
  1.5 0.7 %copy-done.1 = bf16[2,32,64]{2,1,0:T(8,128)(2,1)S(1)} copy-done((bf16[2,32,64]{2,1,0:T(8,128)(2,1)S(1)}, bf16[2,32,64]{2,1,0:T(8,128)(2,1)}, u32[]{:S(2)}) %copy-start.1) | copy-done | bytes 8216
  2.2 0.0 copy-start.2
  2.2 0.7 %copy-done.2 = s32[1,16,32]{2,1,0:T(8,128)S(1)} copy-done((s32[1,16,32]{2,1,0:T(8,128)S(1)}, s32[1,16,32]{2,1,0:T(8,128)}, u32[]{:S(2)}) %copy-start.2) | copy-done | bytes 2072
  2.9 0.0 copy-start.3
  2.9 0.7 %copy-done.3 = s32[8]{0:T(128)S(1)} copy-done((s32[8]{0:T(128)S(1)}, s32[8]{0:T(128)}, u32[]{:S(2)}) %copy-start.3) | copy-done | bytes 56
  3.5 0.0 copy-start.4
  3.5 0.7 %copy-done.4 = f32[2]{0:T(128)S(1)} copy-done((f32[2]{0:T(128)S(1)}, f32[2]{0:T(128)}, u32[]{:S(2)}) %copy-start.4) | copy-done | bytes 32
  4.2 0.0 copy-start.5
  4.2 0.7 %copy-done.5 = f32[3]{0:T(128)S(1)} copy-done((f32[3]{0:T(128)S(1)}, f32[3]{0:T(128)}, u32[]{:S(2)}) %copy-start.5) | copy-done | bytes 36
  4.9 0.0 copy-start.6
  4.9 0.7 %copy-done.6 = f32[3]{0:T(128)S(1)} copy-done((f32[3]{0:T(128)S(1)}, f32[3]{0:T(128)}, u32[]{:S(2)}) %copy-start.6) | copy-done | bytes 36
  5.5 10.9 %shard_map.86 = (f32[4,8,128]{2,1,0:T(8,128)S(1)}, f32[1,64,128]{2,1,0:T(8,128)S(1)}) custom-call(bf16[2,32,64]{2,1,0:T(8,128)(2,1)S(1)} %copy-done.1, bf16[4,64,128]{2,1,0:T(8,128)(2,1)S(1)} %copy-done, s32[1,16,32]{2,1,0:T(8,128)S(1)} %copy-done.2, s32[8]{0:T(128)S(1)} %copy-done.3, f32[2]{0:T(128)S(1)} %copy-done.4, f32[3]{0:T(128)S(1)} %copy-done.5, ...), custom_call_target="tpu_custom_call" | custom-call | tf_op jit(solution)/shard_map/pallas_call | solution.py:357
  16.4 0.6 %copy.11 = f32[4,8,128]{2,1,0:T(8,128)} copy(f32[4,8,128]{2,1,0:T(8,128)S(1)} %get-tuple-element.4) | data formatting | bytes 32768
  17.1 0.6 %copy.12 = f32[1,64,128]{2,1,0:T(8,128)} copy(f32[1,64,128]{2,1,0:T(8,128)S(1)} %get-tuple-element.5) | data formatting | bytes 65536
Async XLA Ops:
  0.6 0.8 %copy-start = (bf16[4,64,128]{2,1,0:T(8,128)(2,1)S(1)}, bf16[4,64,128]{2,1,0:T(8,128)(2,1)}, u32[]{:S(2)}) copy-start(bf16[4,64,128]{2,1,0:T(8,128)(2,1)} %residual_in.1) | copy-start | bytes 196612
  1.5 0.7 %copy-start.1 = (bf16[2,32,64]{2,1,0:T(8,128)(2,1)S(1)}, bf16[2,32,64]{2,1,0:T(8,128)(2,1)}, u32[]{:S(2)}) copy-start(bf16[2,32,64]{2,1,0:T(8,128)(2,1)} %coarse_in.1) | copy-start | bytes 24580
  2.2 0.7 %copy-start.2 = (s32[1,16,32]{2,1,0:T(8,128)S(1)}, s32[1,16,32]{2,1,0:T(8,128)}, u32[]{:S(2)}) copy-start(s32[1,16,32]{2,1,0:T(8,128)} %levels_in.1) | copy-start | bytes 6148
  2.9 0.7 %copy-start.3 = (s32[8]{0:T(128)S(1)}, s32[8]{0:T(128)}, u32[]{:S(2)}) copy-start(s32[8]{0:T(128)} %rank_in.1) | copy-start | bytes 100
  3.5 0.7 %copy-start.4 = (f32[2]{0:T(128)S(1)}, f32[2]{0:T(128)}, u32[]{:S(2)}) copy-start(f32[2]{0:T(128)} %angles_in.1) | copy-start | bytes 28
  4.2 0.7 %copy-start.5 = (f32[3]{0:T(128)S(1)}, f32[3]{0:T(128)}, u32[]{:S(2)}) copy-start(f32[3]{0:T(128)} %slope_in.1) | copy-start | bytes 40
  4.9 0.7 %copy-start.6 = (f32[3]{0:T(128)S(1)}, f32[3]{0:T(128)}, u32[]{:S(2)}) copy-start(f32[3]{0:T(128)} %shift_in.1) | copy-start | bytes 40

commit v2 on v1

--- a/solution.py
+++ b/solution.py
@@ -50,8 +50,8 @@
     angles_in,
     slope_in,
     shift_in,
-    image_out,
-    shade_out,
+    image,
+    shade_sum,
     coarse,
     residual,
     levels,
@@ -72,14 +72,11 @@
     tinted,
     pieces,
     arrived,
-    shade_sum,
-    image,
     load_sem,
     halo_send,
     halo_recv,
     piece_send,
     piece_recv,
-    out_sem,
 ):
     dep, rows, cols = residual.shape
     me = lax.axis_index("depth")
@@ -319,8 +316,6 @@
     others = [lax.rem(me + k, slabs) for k in range(1, slabs)]
     for other in others:
         piece_copy(other, me).start()
-    shade_copy = pltpu.make_async_copy(shade_sum, shade_out, out_sem.at[0])
-    shade_copy.start()
     arrived[me] = pieces[me]
     for other in others:
         piece_copy(other, other).wait_recv()
@@ -335,14 +330,10 @@
     for k in range(3):
         image[k] = total[k]
     image[3] = 1.0 - through
-    image_copy = pltpu.make_async_copy(image, image_out, out_sem.at[1])
-    image_copy.start()
     for copy, allowed in zip(copies, can_send):
         pl.when(allowed)(copy.wait_send)
     for other in others:
         piece_copy(other, me).wait_send()
-    shade_copy.wait()
-    image_copy.wait()
 
 
 def shards(coarse, residual, levels, slab_rank, light_angles, color_slope, color_shift):
@@ -352,16 +343,17 @@
     n_chunks = rows // SUB
     n_blocks = n_chunks // min(n_chunks, cols // 4 // dep)
     f32, bf16 = jnp.float32, jnp.bfloat16
-    hbm = pl.BlockSpec(memory_space=pl.ANY)
+    hbm = pl.BlockSpec(memory_space=pltpu.HBM)
+    vmem = pl.BlockSpec(memory_space=pltpu.VMEM)
     dma = pltpu.SemaphoreType.DMA
     return pl.pallas_call(
         functools.partial(kernel, slabs, tiles),
         out_shape=(
-            jax.ShapeDtypeStruct((4, row_dev, cols), f32),
-            jax.ShapeDtypeStruct((1, rows, cols), f32),
+            pltpu.VMEM((4, row_dev, cols), f32),
+            pltpu.VMEM((1, rows, cols), f32),
         ),
         in_specs=[hbm] * 7,
-        out_specs=(hbm, hbm),
+        out_specs=(vmem, vmem),
         scratch_shapes=[
             pltpu.VMEM(coarse.shape, bf16),
             pltpu.VMEM(residual.shape, bf16),
@@ -383,19 +375,21 @@
             pltpu.VMEM((3, dep, rows, cols), f32),
             pltpu.VMEM((slabs, 4, row_dev, cols), f32),
             pltpu.VMEM((slabs, 4, row_dev, cols), f32),
-            pltpu.VMEM((1, rows, cols), f32),
-            pltpu.VMEM((4, row_dev, cols), f32),
             dma((7,)),
             dma((4,)),
             dma((4,)),
             dma((slabs,)),
             dma((slabs,)),
-            dma((2,)),
         ],
         compiler_params=pltpu.CompilerParams(
             collective_id=0, has_side_effects=True, vmem_limit_bytes=40 * 1024 * 1024
         ),
-    )(coarse, residual, levels, slab_rank, light_angles, color_slope, color_shift)
+    )(
+        *[
+            pltpu.with_memory_space_constraint(x, pltpu.HBM)
+            for x in (coarse, residual, levels, slab_rank, light_angles, color_slope, color_shift)
+        ]
+    )
 
 
 def solution(mesh):

time: 18 us -> 13 us (0.72); the launches traced: 17.7 us -> 12.9 us
  local copies, waits for them, and re-layouts: 6.09 us -> 1.22 us
    unnamed x16 -> x2, local copies, waits for them, and re-layouts: 6.09 us -> 1.22 us
where the time goes in v2:
time: 13 us; the launch traced here: 12.9 us
  Pallas kernels  11 us (85%)
  local copies, waits for them, and re-layouts  1.22 us (9%)
  between operations  0.64 us (5%)
    pallas_call x1, Pallas kernels, shards(): pl.pallas_call(functools.partial(kernel, slabs, tiles), out_shape=(pltpu....  11 us
    unnamed x2, local copies, waits for them, and re-layouts  1.22 us

profile of v2, /device:TPU:0, one launch (start us, length us, event | category | flops | bytes accessed | tf_op | source)
XLA Modules:
  0.0 12.9 jit_solution(9716769659101440458)
XLA Ops:
  0.6 11.0 %shard_map.86 = (f32[4,8,128]{2,1,0:T(8,128)S(1)}, f32[1,64,128]{2,1,0:T(8,128)S(1)}) custom-call(bf16[2,32,64]{2,1,0:T(8,128)(2,1)} %coarse_in.1, bf16[4,64,128]{2,1,0:T(8,128)(2,1)} %residual_in.1, s32[1,16,32]{2,1,0:T(8,128)} %levels_in.1, s32[8]{0:T(128)} %rank_in.1, f32[2]{0:T(128)} %angles_in.1, f32[3]{0:T(128)} %slope_in.1, f32[3]{0:T(128)} %shift_in.1), custom_call_target="tpu_custom_call" | custom-call | tf_op jit(solution)/shard_map/pallas_call | solution.py:349
  11.6 0.6 %copy.11 = f32[4,8,128]{2,1,0:T(8,128)} copy(f32[4,8,128]{2,1,0:T(8,128)S(1)} %get-tuple-element.2) | data formatting | bytes 32768
  12.2 0.6 %copy.12 = f32[1,64,128]{2,1,0:T(8,128)} copy(f32[1,64,128]{2,1,0:T(8,128)S(1)} %get-tuple-element.3) | data formatting | bytes 65536

commit v3 on v2

--- a/solution.py
+++ b/solution.py
@@ -89,27 +89,6 @@
     block = inner * SUB
     step = 4.0 / (dep * slabs)
 
-    barrier = pltpu.get_barrier_semaphore()
-    for k in range(1, slabs):
-        pl.semaphore_signal(
-            barrier,
-            inc=1,
-            device_id=(lax.rem(me + k, slabs), tile),
-            device_id_type=pl.DeviceIdType.MESH,
-        )
-
-    @pl.when(tile > 0)
-    def _():
-        pl.semaphore_signal(
-            barrier, inc=1, device_id=(me, tile - 1), device_id_type=pl.DeviceIdType.MESH
-        )
-
-    @pl.when(tile < tiles - 1)
-    def _():
-        pl.semaphore_signal(
-            barrier, inc=1, device_id=(me, tile + 1), device_id_type=pl.DeviceIdType.MESH
-        )
-
     loads = [
         pltpu.make_async_copy(source, target, load_sem.at[i])
         for i, (source, target) in enumerate(
@@ -124,7 +103,31 @@
             ]
         )
     ]
-    for load in loads:
+    for load in loads[:3]:
+        load.start()
+
+    barrier = pltpu.get_barrier_semaphore()
+    for k in range(1, slabs):
+        pl.semaphore_signal(
+            barrier,
+            inc=1,
+            device_id=(lax.rem(me + k, slabs), tile),
+            device_id_type=pl.DeviceIdType.MESH,
+        )
+
+    @pl.when(tile > 0)
+    def _():
+        pl.semaphore_signal(
+            barrier, inc=1, device_id=(me, tile - 1), device_id_type=pl.DeviceIdType.MESH
+        )
+
+    @pl.when(tile < tiles - 1)
+    def _():
+        pl.semaphore_signal(
+            barrier, inc=1, device_id=(me, tile + 1), device_id_type=pl.DeviceIdType.MESH
+        )
+
+    for load in loads[3:]:
         load.start()
 
     up_c = repeat_matrix((coarse.shape[2], cols), 1)
@@ -136,7 +139,7 @@
     for z in range(dep):
         field[HALO + z, pl.ds(0, SUB), :] = jnp.zeros((SUB, cols), jnp.float32)
         field[HALO + z, pl.ds(SUB + rows, SUB), :] = jnp.zeros((SUB, cols), jnp.float32)
-    for load in loads[1:]:
+    for load in loads[1:3]:
         load.wait()
     lifted = [
         matmul(up_r, matmul(coarse[z], up_c).astype(jnp.bfloat16)) for z in range(coarse.shape[0])
@@ -208,6 +211,8 @@
         def _():
             target[...] = jnp.zeros(target.shape, target.dtype)
 
+    for load in loads[3:]:
+        load.wait()
     ascending = rank[0] < rank[slabs - 1]
     visible = jnp.where(rank[me] >= 0, 1.0, 0.0)
     azimuth = jnp.full((SUB, cols), angles[0], jnp.float32)
@@ -336,6 +341,17 @@
         piece_copy(other, me).wait_send()
 
 
+def store(image, shade, image_out, shade_out, sem):
+    copies = [
+        pltpu.make_async_copy(image, image_out, sem.at[0]),
+        pltpu.make_async_copy(shade, shade_out, sem.at[1]),
+    ]
+    for copy in copies:
+        copy.start()
+    for copy in copies:
+        copy.wait()
+
+
 def shards(coarse, residual, levels, slab_rank, light_angles, color_slope, color_shift):
     dep, rows, cols = residual.shape
     slabs, tiles = lax.axis_size("depth"), lax.axis_size("tile")
@@ -346,7 +362,7 @@
     hbm = pl.BlockSpec(memory_space=pltpu.HBM)
     vmem = pl.BlockSpec(memory_space=pltpu.VMEM)
     dma = pltpu.SemaphoreType.DMA
-    return pl.pallas_call(
+    image, shade = pl.pallas_call(
         functools.partial(kernel, slabs, tiles),
         out_shape=(
             pltpu.VMEM((4, row_dev, cols), f32),
@@ -390,6 +406,13 @@
             for x in (coarse, residual, levels, slab_rank, light_angles, color_slope, color_shift)
         ]
     )
+    return pl.pallas_call(
+        store,
+        out_shape=(pltpu.HBM(image.shape, f32), pltpu.HBM(shade.shape, f32)),
+        in_specs=[vmem] * 2,
+        out_specs=(hbm, hbm),
+        scratch_shapes=[dma((2,))],
+    )(*[pltpu.with_memory_space_constraint(x, pltpu.VMEM) for x in (image, shade)])
 
 
 def solution(mesh):

time: 13 us -> 12.4 us (0.954)
  local copies, waits for them, and re-layouts: 1.22 us -> 0 us
  Pallas kernels: 11 us -> 11.6 us
    unnamed x2 -> x0, local copies, waits for them, and re-layouts: 1.22 us -> none
    pallas_call x0 -> x1, Pallas kernels: none -> 0.64 us  [shards(): pl.pallas_call(store, out_shape=(pltpu.HBM(image.shape, f32), pltpu.HBM(s...]
where the time goes in v3:
time: 12.4 us; the launch traced here: 12.3 us
  Pallas kernels  11.6 us (94%)
  between operations  0.64 us (5%)
    pallas_call x1, Pallas kernels, shards(): pl.pallas_call(functools.partial(kernel, slabs, tiles), out_shape=(pltpu....  11 us
    pallas_call x1, Pallas kernels, shards(): pl.pallas_call(store, out_shape=(pltpu.HBM(image.shape, f32), pltpu.HBM(s...  0.64 us

profile of v3, /device:TPU:0, one launch (start us, length us, event | category | flops | bytes accessed | tf_op | source)
XLA Modules:
  0.0 12.3 jit_solution(3787883394632902994)
XLA Ops:
  0.6 11.0 %shard_map.86 = (f32[4,8,128]{2,1,0:T(8,128)S(1)}, f32[1,64,128]{2,1,0:T(8,128)S(1)}) custom-call(bf16[2,32,64]{2,1,0:T(8,128)(2,1)} %coarse_in.1, bf16[4,64,128]{2,1,0:T(8,128)(2,1)} %residual_in.1, s32[1,16,32]{2,1,0:T(8,128)} %levels_in.1, s32[8]{0:T(128)} %rank_in.1, f32[2]{0:T(128)} %angles_in.1, f32[3]{0:T(128)} %slope_in.1, f32[3]{0:T(128)} %shift_in.1), custom_call_target="tpu_custom_call" | custom-call | tf_op jit(solution)/shard_map/pallas_call | solution.py:365
  11.6 0.6 %shard_map.87 = (f32[4,8,128]{2,1,0:T(8,128)}, f32[1,64,128]{2,1,0:T(8,128)}) custom-call(f32[4,8,128]{2,1,0:T(8,128)S(1)} %get-tuple-element.4.image, f32[1,64,128]{2,1,0:T(8,128)S(1)} %get-tuple-element.5.shade), custom_call_target="tpu_custom_call" | custom-call | tf_op jit(solution)/shard_map/pallas_call | solution.py:409

commit v4 on v3

--- a/solution.py
+++ b/solution.py
@@ -34,6 +34,25 @@
     value = jnp.where(apart == 1, 8.0, value)
     value = jnp.where(apart == 2, -1.0, value)
     return value.astype(jnp.bfloat16)
+
+
+def root(x):
+    return x * lax.rsqrt(jnp.maximum(x, 1e-30))
+
+
+def coded(value):
+    level = root(root(value)) * 65535.0 + 0.5
+    return jnp.minimum(level, 65535.0).astype(jnp.int32)
+
+
+def pair_up(first, second):
+    return (coded(first) << 16) | coded(second)
+
+
+def decoded(word):
+    halves = ((word >> 16) & 65535, word & 65535)
+    roots = [half.astype(jnp.float32) * (1.0 / 65535.0) for half in halves]
+    return [(r * r) * (r * r) for r in roots]
 
 
 def matmul(a, b):
@@ -70,6 +89,7 @@
     grad_y,
     grad_z,
     tinted,
+    veil,
     pieces,
     arrived,
     load_sem,
@@ -251,10 +271,7 @@
                 for k in range(3):
                     colour = 0.5 + 0.5 * jnp.tanh(0.5 * (slope[k] * value[z] + shift[k]))
                     tinted[k, z, here, :] = weight * colour
-            chunk = q * inner + i
-            pieces[chunk // per_piece, 3, pl.ds(chunk % per_piece * SUB, SUB), :] = (
-                1.0 - up[dep - 1] * passed[dep - 1]
-            ) * visible
+            veil[here, :] = (1.0 - up[dep - 1] * passed[dep - 1]) * visible
 
     each(n_blocks, halo_free)
 
@@ -302,9 +319,12 @@
                 shades.append(0.25 + 0.75 * jnp.abs(along) * lax.rsqrt(square))
             shade_sum[0, here, :] = sum(shades) * (1.0 / dep)
             chunk = q * inner + i
-            for k in range(3):
-                total = sum(tinted[k, z, here, :] * shades[z] for z in range(dep))
-                pieces[chunk // per_piece, k, pl.ds(chunk % per_piece * SUB, SUB), :] = total
+            totals = [sum(tinted[k, z, here, :] * shades[z] for z in range(dep)) for k in range(3)]
+            totals.append(veil[here, :])
+            for k in range(2):
+                pieces[chunk // per_piece, k, pl.ds(chunk % per_piece * SUB, SUB), :] = pair_up(
+                    totals[2 * k], totals[2 * k + 1]
+                )
 
     each(n_blocks, finish)
 
@@ -327,9 +347,10 @@
     total = [jnp.zeros((row_dev, cols), jnp.float32) for _ in range(3)]
     through = jnp.ones((row_dev, cols), jnp.float32)
     for s in range(slabs):
-        layer = [
-            jnp.where(ascending, arrived[s, k], arrived[slabs - 1 - s, k]) for k in range(4)
+        words = [
+            jnp.where(ascending, arrived[s, k], arrived[slabs - 1 - s, k]) for k in range(2)
         ]
+        layer = decoded(words[0]) + decoded(words[1])
         total = [total[k] + through * layer[k] for k in range(3)]
         through = through * (1.0 - layer[3])
     for k in range(3):
@@ -389,8 +410,9 @@
             pltpu.VMEM((dep, rows, cols), f32),
             pltpu.VMEM((dep, rows, cols), f32),
             pltpu.VMEM((3, dep, rows, cols), f32),
-            pltpu.VMEM((slabs, 4, row_dev, cols), f32),
-            pltpu.VMEM((slabs, 4, row_dev, cols), f32),
+            pltpu.VMEM((rows, cols), f32),
+            pltpu.VMEM((slabs, 2, row_dev, cols), jnp.int32),
+            pltpu.VMEM((slabs, 2, row_dev, cols), jnp.int32),
             dma((7,)),
             dma((4,)),
             dma((4,)),

time: 12.4 us -> 12.4 us (level)
  no operation moved by 1% of the time
where the time goes in v4:
time: 12.4 us; the launch traced here: 12.3 us
  Pallas kernels  11.6 us (94%)
  between operations  0.64 us (5%)
    pallas_call x1, Pallas kernels, shards(): pl.pallas_call(functools.partial(kernel, slabs, tiles), out_shape=(pltpu....  11 us
    pallas_call x1, Pallas kernels, shards(): pl.pallas_call(store, out_shape=(pltpu.HBM(image.shape, f32), pltpu.HBM(s...  0.64 us

profile of v4, /device:TPU:0, one launch (start us, length us, event | category | flops | bytes accessed | tf_op | source)
XLA Modules:
  0.0 12.3 jit_solution(1477401628026537155)
XLA Ops:
  0.6 11.0 %shard_map.86 = (f32[4,8,128]{2,1,0:T(8,128)S(1)}, f32[1,64,128]{2,1,0:T(8,128)S(1)}) custom-call(bf16[2,32,64]{2,1,0:T(8,128)(2,1)} %coarse_in.1, bf16[4,64,128]{2,1,0:T(8,128)(2,1)} %residual_in.1, s32[1,16,32]{2,1,0:T(8,128)} %levels_in.1, s32[8]{0:T(128)} %rank_in.1, f32[2]{0:T(128)} %angles_in.1, f32[3]{0:T(128)} %slope_in.1, f32[3]{0:T(128)} %shift_in.1), custom_call_target="tpu_custom_call" | custom-call | tf_op jit(solution)/shard_map/pallas_call | solution.py:386
  11.6 0.6 %shard_map.87 = (f32[4,8,128]{2,1,0:T(8,128)}, f32[1,64,128]{2,1,0:T(8,128)}) custom-call(f32[4,8,128]{2,1,0:T(8,128)S(1)} %get-tuple-element.4.image, f32[1,64,128]{2,1,0:T(8,128)S(1)} %get-tuple-element.5.shade), custom_call_target="tpu_custom_call" | custom-call | tf_op jit(solution)/shard_map/pallas_call | solution.py:431

commit v5 on v4

--- a/solution.py
+++ b/solution.py
@@ -127,7 +127,8 @@
         load.start()
 
     barrier = pltpu.get_barrier_semaphore()
-    for k in range(1, slabs):
+    order = sorted(range(1, slabs), key=lambda k: min(k, slabs - k))
+    for k in order:
         pl.semaphore_signal(
             barrier,
             inc=1,
@@ -277,6 +278,16 @@
 
     for copy, allowed in zip(copies, can_take):
         pl.when(allowed)(copy.wait_recv)
+
+    def piece_copy(other, slot):
+        return pltpu.make_async_remote_copy(
+            pieces.at[other],
+            arrived.at[slot],
+            piece_send.at[other],
+            piece_recv.at[slot],
+            device_id=(other, tile),
+            device_id_type=pl.DeviceIdType.MESH,
+        )
 
     def finish(q):
         left, right = edge_left[q], edge_right[q]
@@ -325,22 +336,13 @@
                 pieces[chunk // per_piece, k, pl.ds(chunk % per_piece * SUB, SUB), :] = pair_up(
                     totals[2 * k], totals[2 * k + 1]
                 )
+            if (i + 1) % per_piece == 0:
+                piece = chunk // per_piece
+                pl.when(piece != me)(piece_copy(piece, me).start)
 
     each(n_blocks, finish)
 
-    def piece_copy(other, slot):
-        return pltpu.make_async_remote_copy(
-            pieces.at[other],
-            arrived.at[slot],
-            piece_send.at[other],
-            piece_recv.at[slot],
-            device_id=(other, tile),
-            device_id_type=pl.DeviceIdType.MESH,
-        )
-
     others = [lax.rem(me + k, slabs) for k in range(1, slabs)]
-    for other in others:
-        piece_copy(other, me).start()
     arrived[me] = pieces[me]
     for other in others:
         piece_copy(other, other).wait_recv()

time: 12.4 us -> 12.3 us (level)
  no operation moved by 1% of the time
where the time goes in v5:
time: 12.3 us; the launch traced here: 12.2 us
  Pallas kernels  11.5 us (93%)
  between operations  0.64 us (5%)
    pallas_call x1, Pallas kernels, shards(): pl.pallas_call(functools.partial(kernel, slabs, tiles), out_shape=(pltpu....  10.9 us
    pallas_call x1, Pallas kernels, shards(): pl.pallas_call(store, out_shape=(pltpu.HBM(image.shape, f32), pltpu.HBM(s...  0.64 us

profile of v5, /device:TPU:0, one launch (start us, length us, event | category | flops | bytes accessed | tf_op | source)
XLA Modules:
  0.0 12.2 jit_solution(18368654411220880821)
XLA Ops:
  0.6 10.9 %shard_map.86 = (f32[4,8,128]{2,1,0:T(8,128)S(1)}, f32[1,64,128]{2,1,0:T(8,128)S(1)}) custom-call(bf16[2,32,64]{2,1,0:T(8,128)(2,1)} %coarse_in.1, bf16[4,64,128]{2,1,0:T(8,128)(2,1)} %residual_in.1, s32[1,16,32]{2,1,0:T(8,128)} %levels_in.1, s32[8]{0:T(128)} %rank_in.1, f32[2]{0:T(128)} %angles_in.1, f32[3]{0:T(128)} %slope_in.1, f32[3]{0:T(128)} %shift_in.1), custom_call_target="tpu_custom_call" | custom-call | tf_op jit(solution)/shard_map/pallas_call | solution.py:388
  11.5 0.6 %shard_map.87 = (f32[4,8,128]{2,1,0:T(8,128)}, f32[1,64,128]{2,1,0:T(8,128)}) custom-call(f32[4,8,128]{2,1,0:T(8,128)S(1)} %get-tuple-element.4.image, f32[1,64,128]{2,1,0:T(8,128)S(1)} %get-tuple-element.5.shade), custom_call_target="tpu_custom_call" | custom-call | tf_op jit(solution)/shard_map/pallas_call | solution.py:433

commit v6 on v3

v6 whole, which is shorter than its diff:
```python
import functools

import jax
import jax.numpy as jnp
from jax import lax
from jax.experimental import pallas as pl
from jax.experimental.pallas import tpu as pltpu
from jax.sharding import PartitionSpec as P

SUB = 8
HALO = 2


def each(count, body):
    if count == 1:
        body(0)
    else:
        lax.fori_loop(0, count, lambda i, _: (body(i), 0)[1], 0)


def repeat_matrix(shape, dim):
    factor = shape[dim] // shape[1 - dim]
    long = lax.broadcasted_iota(jnp.int32, shape, dim)
    short = lax.broadcasted_iota(jnp.int32, shape, 1 - dim) * factor
    return ((long >= short) & (long < short + factor)).astype(jnp.float32).astype(jnp.bfloat16)


def stencil_matrix(cols):
    apart = lax.broadcasted_iota(jnp.int32, (cols, cols), 0) - lax.broadcasted_iota(
        jnp.int32, (cols, cols), 1
    )
    value = jnp.where(apart == -2, 1.0, 0.0)
    value = jnp.where(apart == -1, -8.0, value)
    value = jnp.where(apart == 1, 8.0, value)
    value = jnp.where(apart == 2, -1.0, value)
    return value.astype(jnp.bfloat16)


def matmul(a, b):
    return jnp.dot(a, b, preferred_element_type=jnp.float32)


def edge_terms(left, right, lane):
    cols = left.shape[1]
    place = lane & 3
    both = jnp.where(place < 2, left, right)
    outer = jnp.where(place < 2, -pltpu.roll(both, cols - 2, 1), pltpu.roll(both, 2, 1))
    near = jnp.where(
        place == 1,
        pltpu.roll(both, cols - 1, 1),
        jnp.where(place == 2, -pltpu.roll(both, 1, 1), 0.0),
    )
    return outer + 8.0 * near


def kernel(
    slabs,
    tiles,
    coarse_in,
    residual_in,
    levels_in,
    rank_in,
    angles_in,
    slope_in,
    shift_in,
    image,
    shade_sum,
    coarse,
    residual,
    levels,
    rank,
    angles,
    slope,
    shift,
    field16,
    field,
    low_halo,
    high_halo,
    edge,
    edge_left,
    edge_right,
    rows_out,
    rows_left,
    rows_right,
    parts,
    parts_in,
    mine,
    mine_x,
    grad_x,
    grad_y,
    grad_z,
    load_sem,
    halo_send,
    halo_recv,
    part_send,
    part_recv,
    left_send,
    left_recv,
    right_send,
    right_recv,
):
    dep, rows, cols = residual.shape
    me = lax.axis_index("depth")
    tile = lax.axis_index("tile")
    n_chunks = rows // SUB
    inner = min(n_chunks, cols // 4 // dep)
    n_blocks = n_chunks // inner
    block = inner * SUB
    main = dep * SUB
    step = 4.0 / (dep * slabs)
    mesh_id = pl.DeviceIdType.MESH
    has_left, has_right = tile > 0, tile < tiles - 1

    loads = [
        pltpu.make_async_copy(source, target, load_sem.at[i])
        for i, (source, target) in enumerate(
            [
                (residual_in, residual),
                (coarse_in, coarse),
                (levels_in, levels),
                (rank_in, rank),
                (angles_in, angles),
                (slope_in, slope),
                (shift_in, shift),
            ]
        )
    ]
    for load in loads[:3]:
        load.start()

    barrier = pltpu.get_barrier_semaphore()
    for k in range(1, slabs):
        pl.semaphore_signal(
            barrier, inc=1, device_id=(lax.rem(me + k, slabs), tile), device_id_type=mesh_id
        )
    for allowed, to in ((has_left, tile - 1), (has_right, tile + 1)):

        @pl.when(allowed)
        def _():
            for k in range(slabs):
                p = lax.rem(me + k, slabs)
                pl.semaphore_signal(barrier, inc=1, device_id=(p, to), device_id_type=mesh_id)

    for load in loads[3:]:
        load.start()

    up_c = repeat_matrix((coarse.shape[2], cols), 1)
    up_r = repeat_matrix((rows, coarse.shape[1]), 0)
    level_c = repeat_matrix((levels.shape[2], cols), 1)
    level_r = repeat_matrix((rows, levels.shape[1]), 0)
    stencil = stencil_matrix(cols)
    lane = lax.broadcasted_iota(jnp.int32, (SUB, cols), 1)
    row = lax.broadcasted_iota(jnp.int32, (SUB, cols), 0)
    zero = jnp.zeros((SUB, cols), jnp.float32)
    for z in range(dep):
        field[z, pl.ds(0, SUB), :] = zero
        field[z, pl.ds(SUB + rows, SUB), :] = zero
    for g in (0, 1, HALO + slabs * dep, HALO + slabs * dep + 1):
        mine[g, pl.ds(SUB, SUB), :] = zero
    for load in loads[1:3]:
        load.wait()
    lifted = [
        matmul(up_r, matmul(coarse[z], up_c).astype(jnp.bfloat16)) for z in range(coarse.shape[0])
    ]
    scaled = [
        matmul(
            level_r,
            matmul((0.5 * levels[z].astype(jnp.float32)).astype(jnp.bfloat16), level_c).astype(
                jnp.bfloat16
            ),
        )
        for z in range(levels.shape[0])
    ]
    loads[0].wait()
    for z in range(dep):
        value = lifted[z * coarse.shape[0] // dep] + scaled[
            z * levels.shape[0] // dep
        ] * residual[z].astype(jnp.float32)
        rounded = value.astype(jnp.bfloat16)
        field16[z] = rounded
        field[z, pl.ds(SUB, rows), :] = rounded.astype(jnp.float32)

    def rows_of(q, i):
        start = q * block + i * SUB
        return start if isinstance(start, int) else pl.multiple_of(start, SUB)

    def pack(q):
        packed = zero
        for i in range(inner):
            start = rows_of(q, i)
            piece = q * inner + i

            def rows_at(z, offset):
                return field[z, pl.ds(SUB + start + offset, SUB), :]

            strips = []
            for z in range(0, dep, 2):
                for other in range(2):
                    j = i * dep + z + other
                    turned = pltpu.roll(rows_at(z + other, 0), (4 * j + HALO) % cols, 1)
                    packed = jnp.where((lane >> 2) == j, turned, packed)
                pair = jnp.concatenate([rows_at(z, 0), rows_at(z + 1, 0)], axis=0)
                parts[piece, z // 2] = pair.astype(jnp.bfloat16)
                strip = jnp.where(row >= 6, rows_at(z, -8), rows_at(z, 8))
                strip = jnp.where((row == 2) | (row == 3), rows_at(z + 1, -4), strip)
                strip = jnp.where((row == 4) | (row == 5), rows_at(z + 1, 4), strip)
                strips.append(strip)
            for k in range(dep // 4):
                pair = jnp.concatenate(strips[2 * k : 2 * k + 2], axis=0)
                parts[piece, dep // 2 + k] = pair.astype(jnp.bfloat16)
        edge[q] = packed
        for i in range(inner):
            rows_out[q * inner + i] = pltpu.roll(packed, -4 * dep * i % cols, 1)

    each(n_blocks, pack)

    copies = [
        pltpu.make_async_remote_copy(
            source, target, halo_send.at[i], halo_recv.at[i], device_id=to, device_id_type=mesh_id
        )
        for i, (source, target, to) in enumerate(
            [
                (field16.at[pl.ds(dep - HALO, HALO)], low_halo, (me + 1, tile)),
                (field16.at[pl.ds(0, HALO)], high_halo, (me - 1, tile)),
                (edge, edge_left, (me, tile + 1)),
                (edge, edge_right, (me, tile - 1)),
            ]
        )
    ]
    can_send = [me < slabs - 1, me > 0, has_right, has_left]
    can_take = [me > 0, me < slabs - 1, has_left, has_right]
    landing = [low_halo, high_halo, edge_left, edge_right]

    def part_copy(other, slot):
        return pltpu.make_async_remote_copy(
            parts.at[other],
            parts_in.at[slot],
            part_send.at[other],
            part_recv.at[slot],
            device_id=(other, tile),
            device_id_type=mesh_id,
        )

    def row_copy(other, slot, to_right, to):
        target, send, recv = (
            (rows_left, left_send, left_recv) if to_right else (rows_right, right_send, right_recv)
        )
        return pltpu.make_async_remote_copy(
            rows_out.at[other],
            target.at[slot],
            send.at[other],
            recv.at[slot],
            device_id=(other, to),
            device_id_type=mesh_id,
        )

    others = [lax.rem(me + k, slabs) for k in range(1, slabs)]
    pl.semaphore_wait(
        barrier,
        slabs - 1 + slabs * (has_left.astype(jnp.int32) + has_right.astype(jnp.int32)),
    )
    for other in others:
        part_copy(other, me).start()
    for to_right, allowed, to in ((True, has_right, tile + 1), (False, has_left, tile - 1)):

        @pl.when(allowed)
        def _():
            for p in [me] + others:
                row_copy(p, me, to_right, to).start()

    for copy, allowed in zip(copies, can_send):
        pl.when(allowed)(copy.start)
    for target, allowed in zip(
        landing + [rows_left, rows_right], can_take + [has_left, has_right]
    ):

        @pl.when(jnp.logical_not(allowed))
        def _():
            target[...] = jnp.zeros(target.shape, target.dtype)

    parts_in[me] = parts[me]
    for load in loads[3:]:
        load.wait()
    ascending = rank[0] < rank[slabs - 1]
    azimuth = jnp.full((SUB, cols), angles[0], jnp.float32)
    elevation = jnp.full((SUB, cols), angles[1], jnp.float32)
    light_z = jnp.sin(elevation)
    light_y = jnp.cos(elevation) * jnp.sin(azimuth)
    light_x = jnp.cos(elevation) * jnp.cos(azimuth)
    at_edge = (lane < HALO) | (lane >= cols - HALO)

    def shading(gz, gy, gx):
        along = light_z * gz + light_y * gy + light_x * gx
        square = gz * gz + gy * gy + gx * gx + 144.0
        return 0.25 + 0.75 * jnp.abs(along) * lax.rsqrt(square)

    def corrected(gx, fix, j):
        return gx + jnp.where(at_edge, pltpu.roll(fix, (cols - HALO - 4 * j) % cols, 1), 0.0)

    for z in range(dep):
        grad_x[z] = matmul(field16[z], stencil)

    def halo_free(q):
        for i in range(inner):
            start = rows_of(q, i)
            here = pl.ds(start, SUB)
            value = [field[z, pl.ds(SUB + start, SUB), :] for z in range(dep)]
            for z in range(dep):

                def at(dy):
                    return field[z, pl.ds(SUB + start + dy, SUB), :]

                grad_y[z, here, :] = (at(-2) - at(2)) + 8.0 * (at(1) - at(-1))
                part = zero
                for dz, factor in ((-2, 1.0), (-1, -8.0), (1, 8.0), (2, -1.0)):
                    if 0 <= z + dz < dep:
                        part = part + factor * value[z + dz]
                grad_z[z, here, :] = part

    each(n_blocks, halo_free)

    for other in others:
        part_copy(other, other).wait_recv()
    for to_right, allowed, to in ((True, has_left, tile - 1), (False, has_right, tile + 1)):

        @pl.when(allowed)
        def _():
            for p in [me] + others:
                row_copy(p, p, to_right, to).wait_recv()

    group = min(slabs, inner)
    n_groups = slabs // group

    def unpack(q):
        for i in range(group):
            s = q * group + i
            values = parts_in[s].astype(jnp.float32).reshape(main * 3 // 2, cols)
            for z in range(dep):
                g = HALO + s * dep + z
                first = main + z // 2 * SUB
                strip = values[first : first + SUB]
                if z % 2:
                    strip = pltpu.roll(strip, 4, 0)
                mine[g, pl.ds(0, SUB), :] = strip
                mine[g, pl.ds(SUB, SUB), :] = values[z * SUB : (z + 1) * SUB]
                mine[g, pl.ds(2 * SUB, SUB), :] = strip
        together = parts_in[pl.ds(q * group, group), pl.ds(0, dep // 2)]
        mine_x[pl.ds(q * group, group)] = matmul(
            together.reshape(group * main, cols), stencil
        ).reshape(group, main, cols)

    each(n_groups, unpack)

    def composite(q, carry):
        total, through = list(carry[:3]), carry[3]
        sides = []
        for arrived in (rows_left, rows_right):
            gathered = zero
            for i in range(group):
                turned = pltpu.roll(arrived[q * group + i], 4 * dep * i % cols, 1)
                gathered = jnp.where(lane // (4 * dep) == i, turned, gathered)
            sides.append(gathered)
        fix = edge_terms(*sides, lane)
        for i in range(group):
            s = q * group + i
            visible = rank[s] >= 0
            for z in range(dep):
                g = HALO + s * dep + z

                def at(dz, dy):
                    return mine[g + dz, pl.ds(SUB + dy, SUB), :]

                value = at(0, 0)
                gz = (at(-2, 0) - at(2, 0)) + 8.0 * (at(1, 0) - at(-1, 0))
                gy = (at(0, -2) - at(0, 2)) + 8.0 * (at(0, 1) - at(0, -1))
                gx = corrected(mine_x[s, pl.ds(z * SUB, SUB), :], fix, i * dep + z)
                passed = jnp.exp(-step * (2.0 + 2.0 * jnp.tanh(1.5 * (value - 1.5))))
                passed = jnp.where(visible, passed, 1.0)
                weight = (1.0 - passed) * shading(gz, gy, gx)
                factor_old = jnp.where(ascending, 1.0, passed)
                factor_new = jnp.where(ascending, through, 1.0) * weight
                for k in range(3):
                    colour = 0.5 + 0.5 * jnp.tanh(0.5 * (slope[k] * value + shift[k]))
                    total[k] = total[k] * factor_old + factor_new * colour
                through = through * passed
        return (*total, through)

    start = (zero, zero, zero, zero + 1.0)
    done = composite(0, start) if n_groups == 1 else lax.fori_loop(0, n_groups, composite, start)
    for k in range(3):
        image[k] = done[k]
    image[3] = 1.0 - done[3]

    for copy, allowed in zip(copies, can_take):
        pl.when(allowed)(copy.wait_recv)

    def finish(q):
        fix = edge_terms(edge_left[q], edge_right[q], lane)
        whole = q * block
        whole = whole if isinstance(whole, int) else pl.multiple_of(whole, block)
        low = [low_halo[z, pl.ds(whole, block), :].astype(jnp.float32) for z in range(HALO)]
        high = [high_halo[z, pl.ds(whole, block), :].astype(jnp.float32) for z in range(HALO)]
        for i in range(inner):
            here = pl.ds(rows_of(q, i), SUB)
            low_i = [v[i * SUB : (i + 1) * SUB] for v in low]
            high_i = [v[i * SUB : (i + 1) * SUB] for v in high]
            shades = []
            for z in range(dep):
                gx = corrected(grad_x[z, here, :], fix, i * dep + z)
                gz = grad_z[z, here, :]
                if z - 2 < 0:
                    gz = gz + low_i[z]
                if z - 1 < 0:
                    gz = gz - 8.0 * low_i[z + 1]
                if z + 1 >= dep:
                    gz = gz + 8.0 * high_i[z + 1 - dep]
                if z + 2 >= dep:
                    gz = gz - high_i[z + 2 - dep]
                shades.append(shading(gz, grad_y[z, here, :], gx))
            shade_sum[0, here, :] = sum(shades) * (1.0 / dep)

    each(n_blocks, finish)

    for copy, allowed in zip(copies, can_send):
        pl.when(allowed)(copy.wait_send)
    for other in others:
        part_copy(other, me).wait_send()
    for to_right, allowed, to in ((True, has_right, tile + 1), (False, has_left, tile - 1)):

        @pl.when(allowed)
        def _():
            for p in [me] + others:
                row_copy(p, me, to_right, to).wait_send()


def store(image, shade, image_out, shade_out, sem):
    copies = [
        pltpu.make_async_copy(image, image_out, sem.at[0]),
        pltpu.make_async_copy(shade, shade_out, sem.at[1]),
    ]
    for copy in copies:
        copy.start()
    for copy in copies:
        copy.wait()


def shards(coarse, residual, levels, slab_rank, light_angles, color_slope, color_shift):
    dep, rows, cols = residual.shape
    slabs, tiles = lax.axis_size("depth"), lax.axis_size("tile")
    row_dev = rows // slabs
    n_chunks = rows // SUB
    n_blocks = n_chunks // min(n_chunks, cols // 4 // dep)
    f32, bf16 = jnp.float32, jnp.bfloat16
    hbm = pl.BlockSpec(memory_space=pltpu.HBM)
    vmem = pl.BlockSpec(memory_space=pltpu.VMEM)
    dma = pltpu.SemaphoreType.DMA
    image, shade = pl.pallas_call(
        functools.partial(kernel, slabs, tiles),
        out_shape=(
            pltpu.VMEM((4, row_dev, cols), f32),
            pltpu.VMEM((1, rows, cols), f32),
        ),
        in_specs=[hbm] * 7,
        out_specs=(vmem, vmem),
        scratch_shapes=[
            pltpu.VMEM(coarse.shape, bf16),
            pltpu.VMEM(residual.shape, bf16),
            pltpu.VMEM(levels.shape, jnp.int32),
            pltpu.SMEM(slab_rank.shape, jnp.int32),
            pltpu.SMEM(light_angles.shape, f32),
            pltpu.SMEM(color_slope.shape, f32),
            pltpu.SMEM(color_shift.shape, f32),
            pltpu.VMEM((dep, rows, cols), bf16),
            pltpu.VMEM((dep, rows + 2 * SUB, cols), f32),
            pltpu.VMEM((HALO, rows, cols), bf16),
            pltpu.VMEM((HALO, rows, cols), bf16),
            pltpu.VMEM((n_blocks, SUB, cols), f32),
            pltpu.VMEM((n_blocks, SUB, cols), f32),
            pltpu.VMEM((n_blocks, SUB, cols), f32),
            pltpu.VMEM((slabs, SUB, cols), f32),
            pltpu.VMEM((slabs, SUB, cols), f32),
            pltpu.VMEM((slabs, SUB, cols), f32),
            pltpu.VMEM((slabs, dep * 3 // 4, 2 * SUB, cols), bf16),
            pltpu.VMEM((slabs, dep * 3 // 4, 2 * SUB, cols), bf16),
            pltpu.VMEM((slabs * dep + 2 * HALO, 4 * SUB, cols), f32),
            pltpu.VMEM((slabs, dep * SUB, cols), f32),
            pltpu.VMEM((dep, rows, cols), f32),
            pltpu.VMEM((dep, rows, cols), f32),
            pltpu.VMEM((dep, rows, cols), f32),
            dma((7,)),
            dma((4,)),
            dma((4,)),
            dma((slabs,)),
            dma((slabs,)),
            dma((slabs,)),
            dma((slabs,)),
            dma((slabs,)),
            dma((slabs,)),
        ],
        compiler_params=pltpu.CompilerParams(
            collective_id=0, has_side_effects=True, vmem_limit_bytes=40 * 1024 * 1024
        ),
    )(
        *[
            pltpu.with_memory_space_constraint(x, pltpu.HBM)
            for x in (coarse, residual, levels, slab_rank, light_angles, color_slope, color_shift)
        ]
    )
    return pl.pallas_call(
        store,
        out_shape=(pltpu.HBM(image.shape, f32), pltpu.HBM(shade.shape, f32)),
        in_specs=[vmem] * 2,
        out_specs=(hbm, hbm),
        scratch_shapes=[dma((2,))],
    )(*[pltpu.with_memory_space_constraint(x, pltpu.VMEM) for x in (image, shade)])


def solution(mesh):
    placed = (
        P("depth", None, "tile"),
        P("depth", None, "tile"),
        P("depth", None, "tile"),
        P(),
        P(),
        P(),
        P(),
    )
    return jax.shard_map(
        shards,
        mesh=mesh,
        in_specs=placed,
        out_specs=(P(None, "depth", "tile"), P("depth", None, "tile")),
        check_vma=False,
    )
```

time: 12.4 us -> 11.2 us (0.903)
  Pallas kernels: 11.6 us -> 10.4 us
    pallas_call x1, Pallas kernels: 11 us -> 9.79 us  [shards(): pl.pallas_call(functools.partial(kernel, slabs, tiles), out_shape=(pltpu....]
where the time goes in v6:
time: 11.2 us; the launch traced here: 11.1 us
  Pallas kernels  10.4 us (93%)
  between operations  0.64 us (6%)
    pallas_call x1, Pallas kernels, shards(): pl.pallas_call(functools.partial(kernel, slabs, tiles), out_shape=(pltpu....  9.79 us
    pallas_call x1, Pallas kernels, shards(): pl.pallas_call(store, out_shape=(pltpu.HBM(image.shape, f32), pltpu.HBM(s...  0.64 us

profile of v6, /device:TPU:0, one launch (start us, length us, event | category | flops | bytes accessed | tf_op | source)
XLA Modules:
  0.0 11.1 jit_solution(16307355706625924786)
XLA Ops:
  0.6 9.8 %shard_map.86 = (f32[4,8,128]{2,1,0:T(8,128)S(1)}, f32[1,64,128]{2,1,0:T(8,128)S(1)}) custom-call(bf16[2,32,64]{2,1,0:T(8,128)(2,1)} %coarse_in.1, bf16[4,64,128]{2,1,0:T(8,128)(2,1)} %residual_in.1, s32[1,16,32]{2,1,0:T(8,128)} %levels_in.1, s32[8]{0:T(128)} %rank_in.1, f32[2]{0:T(128)} %angles_in.1, f32[3]{0:T(128)} %slope_in.1, f32[3]{0:T(128)} %shift_in.1), custom_call_target="tpu_custom_call" | custom-call | tf_op jit(solution)/shard_map/pallas_call | solution.py:457
  10.4 0.6 %shard_map.87 = (f32[4,8,128]{2,1,0:T(8,128)}, f32[1,64,128]{2,1,0:T(8,128)}) custom-call(f32[4,8,128]{2,1,0:T(8,128)S(1)} %get-tuple-element.4.image, f32[1,64,128]{2,1,0:T(8,128)S(1)} %get-tuple-element.5.shade), custom_call_target="tpu_custom_call" | custom-call | tf_op jit(solution)/shard_map/pallas_call | solution.py:509

commit v7 on v6

--- a/solution.py
+++ b/solution.py
@@ -259,6 +259,8 @@
         barrier,
         slabs - 1 + slabs * (has_left.astype(jnp.int32) + has_right.astype(jnp.int32)),
     )
+    for copy, allowed in zip(copies, can_send):
+        pl.when(allowed)(copy.start)
     for other in others:
         part_copy(other, me).start()
     for to_right, allowed, to in ((True, has_right, tile + 1), (False, has_left, tile - 1)):
@@ -268,8 +270,6 @@
             for p in [me] + others:
                 row_copy(p, me, to_right, to).start()
 
-    for copy, allowed in zip(copies, can_send):
-        pl.when(allowed)(copy.start)
     for target, allowed in zip(
         landing + [rows_left, rows_right], can_take + [has_left, has_right]
     ):
@@ -318,78 +318,6 @@
                 grad_z[z, here, :] = part
 
     each(n_blocks, halo_free)
-
-    for other in others:
-        part_copy(other, other).wait_recv()
-    for to_right, allowed, to in ((True, has_left, tile - 1), (False, has_right, tile + 1)):
-
-        @pl.when(allowed)
-        def _():
-            for p in [me] + others:
-                row_copy(p, p, to_right, to).wait_recv()
-
-    group = min(slabs, inner)
-    n_groups = slabs // group
-
-    def unpack(q):
-        for i in range(group):
-            s = q * group + i
-            values = parts_in[s].astype(jnp.float32).reshape(main * 3 // 2, cols)
-            for z in range(dep):
-                g = HALO + s * dep + z
-                first = main + z // 2 * SUB
-                strip = values[first : first + SUB]
-                if z % 2:
-                    strip = pltpu.roll(strip, 4, 0)
-                mine[g, pl.ds(0, SUB), :] = strip
-                mine[g, pl.ds(SUB, SUB), :] = values[z * SUB : (z + 1) * SUB]
-                mine[g, pl.ds(2 * SUB, SUB), :] = strip
-        together = parts_in[pl.ds(q * group, group), pl.ds(0, dep // 2)]
-        mine_x[pl.ds(q * group, group)] = matmul(
-            together.reshape(group * main, cols), stencil
-        ).reshape(group, main, cols)
-
-    each(n_groups, unpack)
-
-    def composite(q, carry):
-        total, through = list(carry[:3]), carry[3]
-        sides = []
-        for arrived in (rows_left, rows_right):
-            gathered = zero
-            for i in range(group):
-                turned = pltpu.roll(arrived[q * group + i], 4 * dep * i % cols, 1)
-                gathered = jnp.where(lane // (4 * dep) == i, turned, gathered)
-            sides.append(gathered)
-        fix = edge_terms(*sides, lane)
-        for i in range(group):
-            s = q * group + i
-            visible = rank[s] >= 0
-            for z in range(dep):
-                g = HALO + s * dep + z
-
-                def at(dz, dy):
-                    return mine[g + dz, pl.ds(SUB + dy, SUB), :]
-
-                value = at(0, 0)
-                gz = (at(-2, 0) - at(2, 0)) + 8.0 * (at(1, 0) - at(-1, 0))
-                gy = (at(0, -2) - at(0, 2)) + 8.0 * (at(0, 1) - at(0, -1))
-                gx = corrected(mine_x[s, pl.ds(z * SUB, SUB), :], fix, i * dep + z)
-                passed = jnp.exp(-step * (2.0 + 2.0 * jnp.tanh(1.5 * (value - 1.5))))
-                passed = jnp.where(visible, passed, 1.0)
-                weight = (1.0 - passed) * shading(gz, gy, gx)
-                factor_old = jnp.where(ascending, 1.0, passed)
-                factor_new = jnp.where(ascending, through, 1.0) * weight
-                for k in range(3):
-                    colour = 0.5 + 0.5 * jnp.tanh(0.5 * (slope[k] * value + shift[k]))
-                    total[k] = total[k] * factor_old + factor_new * colour
-                through = through * passed
-        return (*total, through)
-
-    start = (zero, zero, zero, zero + 1.0)
-    done = composite(0, start) if n_groups == 1 else lax.fori_loop(0, n_groups, composite, start)
-    for k in range(3):
-        image[k] = done[k]
-    image[3] = 1.0 - done[3]
 
     for copy, allowed in zip(copies, can_take):
         pl.when(allowed)(copy.wait_recv)
@@ -420,6 +348,78 @@
             shade_sum[0, here, :] = sum(shades) * (1.0 / dep)
 
     each(n_blocks, finish)
+
+    for other in others:
+        part_copy(other, other).wait_recv()
+    for to_right, allowed, to in ((True, has_left, tile - 1), (False, has_right, tile + 1)):
+
+        @pl.when(allowed)
+        def _():
+            for p in [me] + others:
+                row_copy(p, p, to_right, to).wait_recv()
+
+    group = min(slabs, inner)
+    n_groups = slabs // group
+
+    def unpack(q):
+        for i in range(group):
+            s = q * group + i
+            values = parts_in[s].astype(jnp.float32).reshape(main * 3 // 2, cols)
+            for z in range(dep):
+                g = HALO + s * dep + z
+                first = main + z // 2 * SUB
+                strip = values[first : first + SUB]
+                if z % 2:
+                    strip = pltpu.roll(strip, 4, 0)
+                mine[g, pl.ds(0, SUB), :] = strip
+                mine[g, pl.ds(SUB, SUB), :] = values[z * SUB : (z + 1) * SUB]
+                mine[g, pl.ds(2 * SUB, SUB), :] = strip
+        together = parts_in[pl.ds(q * group, group), pl.ds(0, dep // 2)]
+        mine_x[pl.ds(q * group, group)] = matmul(
+            together.reshape(group * main, cols), stencil
+        ).reshape(group, main, cols)
+
+    each(n_groups, unpack)
+
+    def composite(q, carry):
+        total, through = list(carry[:3]), carry[3]
+        sides = []
+        for arrived in (rows_left, rows_right):
+            gathered = zero
+            for i in range(group):
+                turned = pltpu.roll(arrived[q * group + i], 4 * dep * i % cols, 1)
+                gathered = jnp.where(lane // (4 * dep) == i, turned, gathered)
+            sides.append(gathered)
+        fix = edge_terms(*sides, lane)
+        for i in range(group):
+            s = q * group + i
+            visible = rank[s] >= 0
+            for z in range(dep):
+                g = HALO + s * dep + z
+
+                def at(dz, dy):
+                    return mine[g + dz, pl.ds(SUB + dy, SUB), :]
+
+                value = at(0, 0)
+                gz = (at(-2, 0) - at(2, 0)) + 8.0 * (at(1, 0) - at(-1, 0))
+                gy = (at(0, -2) - at(0, 2)) + 8.0 * (at(0, 1) - at(0, -1))
+                gx = corrected(mine_x[s, pl.ds(z * SUB, SUB), :], fix, i * dep + z)
+                passed = jnp.exp(-step * (2.0 + 2.0 * jnp.tanh(1.5 * (value - 1.5))))
+                passed = jnp.where(visible, passed, 1.0)
+                weight = (1.0 - passed) * shading(gz, gy, gx)
+                factor_old = jnp.where(ascending, 1.0, passed)
+                factor_new = jnp.where(ascending, through, 1.0) * weight
+                for k in range(3):
+                    colour = 0.5 + 0.5 * jnp.tanh(0.5 * (slope[k] * value + shift[k]))
+                    total[k] = total[k] * factor_old + factor_new * colour
+                through = through * passed
+        return (*total, through)
+
+    start = (zero, zero, zero, zero + 1.0)
+    done = composite(0, start) if n_groups == 1 else lax.fori_loop(0, n_groups, composite, start)
+    for k in range(3):
+        image[k] = done[k]
+    image[3] = 1.0 - done[3]
 
     for copy, allowed in zip(copies, can_send):
         pl.when(allowed)(copy.wait_send)

time: 11.2 us -> 11.1 us (level)
  no operation moved by 1% of the time
where the time goes in v7:
time: 11.1 us; the launch traced here: 11 us
  Pallas kernels  10.3 us (93%)
  between operations  0.64 us (6%)
    pallas_call x1, Pallas kernels, shards(): pl.pallas_call(functools.partial(kernel, slabs, tiles), out_shape=(pltpu....  9.68 us
    pallas_call x1, Pallas kernels, shards(): pl.pallas_call(store, out_shape=(pltpu.HBM(image.shape, f32), pltpu.HBM(s...  0.64 us

profile of v7, /device:TPU:0, one launch (start us, length us, event | category | flops | bytes accessed | tf_op | source)
XLA Modules:
  0.0 11.0 jit_solution(15461154747305489780)
XLA Ops:
  0.6 9.7 %shard_map.86 = (f32[4,8,128]{2,1,0:T(8,128)S(1)}, f32[1,64,128]{2,1,0:T(8,128)S(1)}) custom-call(bf16[2,32,64]{2,1,0:T(8,128)(2,1)} %coarse_in.1, bf16[4,64,128]{2,1,0:T(8,128)(2,1)} %residual_in.1, s32[1,16,32]{2,1,0:T(8,128)} %levels_in.1, s32[8]{0:T(128)} %rank_in.1, f32[2]{0:T(128)} %angles_in.1, f32[3]{0:T(128)} %slope_in.1, f32[3]{0:T(128)} %shift_in.1), custom_call_target="tpu_custom_call" | custom-call | tf_op jit(solution)/shard_map/pallas_call | solution.py:457
  10.3 0.6 %shard_map.87 = (f32[4,8,128]{2,1,0:T(8,128)}, f32[1,64,128]{2,1,0:T(8,128)}) custom-call(f32[4,8,128]{2,1,0:T(8,128)S(1)} %get-tuple-element.4.image, f32[1,64,128]{2,1,0:T(8,128)S(1)} %get-tuple-element.5.shade), custom_call_target="tpu_custom_call" | custom-call | tf_op jit(solution)/shard_map/pallas_call | solution.py:509
